TPU v7x, 32 devices: a whole 2x2x4 slice. The times are simulated.
32 devices in a mesh: seq: 4 (over y, x), head: 8 (over z, core).
Axes of the slice: x: 2, y: 2, z: 4, core: 2. Of those that a mesh axis runs over, the one named last changes fastest.
Arguments:
- pre_x: bfloat16 [4096, 8192], P('seq', 'head'), may hold values from -6 to 6
- pre_bc: bfloat16 [4096, 256], P('seq'), may hold values from -6 to 6
- conv_x: float32 [4, 8192], P(None, 'head'), may hold values from -3 to 3
- conv_bc: float32 [4, 256], replicated, may hold values from -3 to 3
- log_decay: float32 [128, 4096], P('head', 'seq'), may hold values from -1.5 to 0
- lengths: int32 [4], replicated, may hold values from 1 to 2048, 4096 in all
- grad_out: bfloat16 [4096, 8192], P('seq', 'head'), may hold values from -0.119628906 to 0.119628906
Outputs:
- grad_pre_x: float32 [4096, 8192], P('seq', 'head')
- grad_pre_bc: float32 [4096, 256], P(('seq', 'head'))
- grad_log_decay: float32 [128, 4096], P('head', 'seq')
Inputs may be any that keep to these rules, and one draw needn't show every extreme that they name: `lengths`: the 4 counts sum to 4096.
All inputs are finite; a program needn't handle non-finite values.
Results may differ from a plain program's by a relative error of at most 0.0003.
Values may be sent and summed in bfloat16 or wider, within the bound.
No kernel may reach another device: no remote copies, remote signals or barrier semaphores. Data moves between devices by JAX's collectives and lax.ppermute only.
A program may use at most 192 MiB of HBM per device.

v0:
```python
import functools
import jax
import jax.numpy as jnp
from jax import lax
from jax.experimental import pallas as pl
from jax.experimental.pallas import tpu as pltpu
from jax.sharding import PartitionSpec as P

P_SIZE = 64
N = 128
K = 4
CHUNK = 64
LANES = 128
f32 = jnp.float32
bf16 = jnp.bfloat16
NN = (((1,), (0,)), ((), ()))
NT = (((1,), (1,)), ((), ()))
TN = (((0,), (0,)), ((), ()))
VMEM_LIMIT = 56 * 1024 * 1024


def split(value):
    high = value.astype(bf16)
    return high, (value - high.astype(f32)).astype(bf16)


def dot(left, right, dims=NN):
    return lax.dot_general(left, right, dims, preferred_element_type=f32)


def thirds(value):
    high, low = split(value)
    return high, low, (value - high.astype(f32) - low.astype(f32)).astype(bf16)


def exact(left, right, dims=NN):
    if isinstance(left, tuple):
        return dot(left[0], right, dims) + dot(left[1], right, dims) + dot(left[2], right, dims)
    return dot(left, right[0], dims) + dot(left, right[1], dims) + dot(left, right[2], dims)


def stack(*parts):
    return jnp.concatenate(parts, axis=0)


def dot3(left, right, dims=NN):
    rows = left[0].shape[0]
    most = dot(stack(*left), right[0], dims)
    return most[:rows] + most[rows:] + dot(left[0], right[1], dims)


def dot3_tn(left, right):
    return dot(stack(left[0], left[1], left[0]), stack(right[0], right[0], right[1]), TN)


def whole_of(parts):
    return parts[0].astype(f32) + parts[1].astype(f32)


def rows_iota(shape):
    return lax.broadcasted_iota(jnp.int32, shape, 0)


def cols_iota(shape):
    return lax.broadcasted_iota(jnp.int32, shape, 1)


def note_of(position, lens_ref):
    first = lens_ref[0]
    second = first + lens_ref[1]
    third = second + lens_ref[2]
    one = lambda flag: jnp.where(flag, 1, 0)
    return one(position >= 0) + one(position >= first) + one(position >= second) + one(
        position >= third
    )


def widen(block, width):
    return block if width == LANES else jnp.concatenate([block] * (width // LANES), axis=1)


def links(first, rows, sign, lens_ref):
    position = first + rows_iota((rows, LANES))
    here = note_of(position, lens_ref)
    return [
        jnp.where(note_of(position + sign * lag, lens_ref) == here, 1.0, 0.0) for lag in range(1, K)
    ]


def conv_tile(ext_ref, taps_ref, first, rows, over, linked, sign):
    total = ext_ref[first : first + rows, over] * taps_ref[K - 1 : K, over]
    for lag in range(1, K):
        moved = first + sign * lag
        tap = taps_ref[K - 1 - lag : K - lag, over]
        tap = tap if linked is None else tap * linked[lag - 1]
        total = total + ext_ref[moved : moved + rows, over] * tap
    return total


def conv_rows(ext_ref, taps_ref, first, rows, width, position, sign, lens_ref, emit):
    begins = [0, lens_ref[0], lens_ref[0] + lens_ref[1], lens_ref[0] + lens_ref[1] + lens_ref[2]]
    near = [(begin > position - K) & (begin < position + rows + K) for begin in begins]
    cut = near[0] | near[1] | near[2] | near[3]

    def body(linked):
        for c in range(0, width, LANES):
            over = slice(c, c + LANES)
            emit(over, conv_tile(ext_ref, taps_ref, first, rows, over, linked, sign))

    @pl.when(cut)
    def _():
        body(links(position, rows, sign, lens_ref))

    @pl.when(jnp.logical_not(cut))
    def _():
        body(None)


def silu_and_slope(u):
    sigma = 1.0 / (1.0 + jnp.exp(-u))
    value = u * sigma
    return value, sigma + value * (1.0 - sigma)


def expander(heads, channels, group):
    row = rows_iota((2 * LANES, channels)) % LANES
    own = cols_iota((2 * LANES, channels)) // P_SIZE
    return jnp.where(row == group * heads + own, 1.0, 0.0).astype(bf16)


def head_summer(channels):
    same = rows_iota((channels, LANES)) // P_SIZE == cols_iota((channels, LANES))
    return jnp.where(same, 1.0, 0.0).astype(bf16)


def scales_kernel(lens_ref, start_ref, log_ref, scale_ref, kappa_ref, through_ref, padded):
    heads, tokens = log_ref.shape
    channels = kappa_ref.shape[1]
    chunks = tokens // CHUNK
    start = start_ref[0]
    padded[...] = jnp.zeros_like(padded)
    for group in range(4):
        padded[group * heads : (group + 1) * heads, :] = log_ref[...]
    size = 2 * LANES
    square = (size, size)
    row, col = rows_iota(square), cols_iota(square)
    same = row // CHUNK == col // CHUNK
    one = lambda flag: jnp.where(flag, 1.0, 0.0)
    inner = one(same & (col <= row)) - one(same & (col % CHUNK < CHUNK // 2))
    sums = stack(inner, one(col <= row), one(col > row), jnp.ones((16, size), f32)).astype(bf16)
    blocks = tokens // size
    parts = thirds(padded[...])
    tables = [
        exact(sums, tuple(part[:, b * size : (b + 1) * size] for part in parts), NT)
        for b in range(blocks)
    ]
    totals = [table[3 * size : 3 * size + 1, :] for table in tables]
    offsets = [jnp.zeros((1, LANES), f32)]
    for total in totals:
        offsets.append(offsets[-1] + total)
    after = jnp.zeros((1, LANES), f32)
    note_before = note_of(start - 1, lens_ref)
    note_last = note_of(start + tokens - 1, lens_ref)
    shape = (size, LANES)
    group = cols_iota(shape) // heads
    for b in reversed(range(blocks)):
        near, ahead, behind = (tables[b][i * size : (i + 1) * size, :] for i in range(3))
        note = note_of(start + b * size + rows_iota(shape), lens_ref)
        power = jnp.where(group == 0, near, -near)
        power = jnp.where(group == 2, ahead + offsets[b], power)
        power = jnp.where(group >= 3, behind + after, power)
        kept = (group < 2) | ((group == 2) & (note == note_before)) | ((group == 3) & (note == note_last))
        after = after + totals[b]
        rows = slice(b * size, (b + 1) * size)
        scale_ref[rows, :LANES], scale_ref[rows, LANES:] = split(jnp.where(kept, jnp.exp(power), 0.0))
    spread = one(
        rows_iota((LANES, channels)) == cols_iota((LANES, channels)) // P_SIZE
    ).astype(bf16)
    half = CHUNK // 2
    chunk = rows_iota((chunks, tokens)) * CHUNK + half
    col = cols_iota((chunks, tokens))
    for place in range(2):
        begin = chunk + place * half
        steps = exact(one((col >= begin) & (col < begin + half)).astype(bf16), parts, NT)
        kappa_ref[place * chunks : (place + 1) * chunks, :] = exact(thirds(jnp.exp(steps)), spread)
    through = jnp.broadcast_to(jnp.exp(offsets[-1]), (8, LANES)) * one(note_before == note_last)
    through_ref[...] = exact(thirds(through), spread)


def tiles(rows, channels, high=64, wide=LANES):
    return [
        (slice(r, r + high), slice(c, c + wide))
        for r in range(0, rows, high)
        for c in range(0, channels, wide)
    ]


def adjoint_kernel(
    lens_ref, start_ref, grad_ref, scale_ref, pre_ref, halo_ref, taps_ref, through_ref,
    hi_ref, lo_ref, slope_ref, rh_ref, rl_ref, gh_ref, gl_ref, send_ref,
    spread, spread_r, entry, near, ext, *, heads
):
    rows, channels = grad_ref.shape
    step = pl.program_id(0)

    @pl.when(step == 0)
    def _():
        spread[...] = expander(heads, channels, 2)
        spread_r[...] = expander(heads, channels, 0)
        send_ref[...] = jnp.zeros_like(send_ref)
        send_ref[N : N + 8, :] = through_ref[...]
        ext[0:8, :] = halo_ref[8:16, channels:].astype(f32)

    @pl.when(step > 0)
    def _():
        ext[0:8, :] = ext[rows : rows + 8, :]

    ext[8:, :] = pre_ref[...].astype(f32)
    scale = scale_ref[...]
    entry[...] = dot(scale, spread[...])
    near[...] = dot(scale, spread_r[...])
    for first in range(0, rows, 64):
        at = slice(first, first + 64)

        def emit(over, u, at=at):
            value, slope_ref[at, over] = silu_and_slope(u)
            hi_ref[at, over], lo_ref[at, over] = split(value)

        place = start_ref[0] + step * rows + first
        conv_rows(ext, taps_ref, 8 + first, 64, 2 * N, place, -1, lens_ref, emit)
    for at, over in tiles(rows, channels):
        grad = grad_ref[at, over].astype(f32)
        gh_ref[at, over], gl_ref[at, over] = split(grad * entry[at, over])
        rh_ref[at, over], rl_ref[at, over] = split(grad * near[at, over])
    send_ref[0:N, :] += dot3_tn((hi_ref[:, N:], lo_ref[:, N:]), (gh_ref[...], gl_ref[...]))


def state_kernel(
    lens_ref, start_ref, pre_ref, halo_ref, taps_ref, scale_ref, hi_ref, lo_ref, through_ref, other_ref,
    slope_ref, qh_ref, ql_ref, xh_ref, xl_ref, own_ref, *refs, heads, count
):
    messages = refs[: count - 1]
    spread, spread_q, leave, near, ext = refs[count - 1 :]
    rows, channels = pre_ref.shape
    step, steps = pl.program_id(0), pl.num_programs(0)

    @pl.when(step == 0)
    def _():
        spread[...] = expander(heads, channels, 3)
        spread_q[...] = expander(heads, channels, 1)
        own_ref[...] = jnp.zeros_like(own_ref)
        own_ref[N : N + 8, :] = through_ref[...]
        ext[0:8, :] = halo_ref[8:16, :channels].astype(f32)

    @pl.when(step > 0)
    def _():
        ext[0:8, :] = ext[rows : rows + 8, :]

    ext[8:, :] = pre_ref[...].astype(f32)
    scale = scale_ref[...]
    leave[...] = dot(scale, spread[...])
    near[...] = dot(scale, spread_q[...])
    for first in range(0, rows, 64):
        at = slice(first, first + 64)

        def emit(over, u, at=at):
            value, slope_ref[at, over] = silu_and_slope(u)
            xh_ref[at, over], xl_ref[at, over] = split(value * leave[at, over])
            qh_ref[at, over], ql_ref[at, over] = split(value * near[at, over])

        place = start_ref[0] + step * rows + first
        conv_rows(ext, taps_ref, 8 + first, 64, channels, place, -1, lens_ref, emit)
    own_ref[0:N, :] += dot3_tn((hi_ref[:, :N], lo_ref[:, :N]), (xh_ref[...], xl_ref[...]))

    @pl.when(step == steps - 1)
    def _():
        for lag in range(1, count):
            ahead = start_ref[0] + lag * rows * steps < count * rows * steps
            messages[lag - 1][...] = jnp.where(ahead, own_ref[...], other_ref[...])


def local_kernel(
    lens_ref, start_ref, kappa_ref,
    fx_h, fx_l, fg_h, fg_l, f_hi, f_lo, bx_h, bx_l, bg_h, bg_l, b_hi, b_lo,
    dx_ref, dbc_ref, rate_ref, state, adjoint, summer, product
):
    step = pl.program_id(0)
    chunks = pl.num_programs(0)
    channels = dx_ref.shape[1]
    here, there = step, chunks - 1 - step

    @pl.when(step == 0)
    def _():
        summer[...] = head_summer(channels)
        state[...] = jnp.zeros_like(state)
        adjoint[...] = jnp.zeros_like(adjoint)
        dbc_ref[...] = jnp.zeros_like(dbc_ref)
        rate_ref[...] = jnp.zeros_like(rate_ref)

    square = (CHUNK, CHUNK)
    row, col = rows_iota(square), cols_iota(square)
    pick = lambda flag, parts: tuple(
        jnp.where(flag, part.astype(f32), 0.0).astype(bf16) for part in parts
    )
    beside = lambda left, right: tuple(jnp.concatenate(p, axis=1) for p in zip(left, right))
    below = lambda left, right: tuple(stack(*p) for p in zip(left, right))
    turned = lambda parts: stack(parts[0], parts[1], parts[0]).astype(f32).T.astype(bf16)

    def setting(chunk, hi_ref, lo_ref):
        first = start_ref[0] + chunk * CHUNK
        note_before = note_of(first - 1, lens_ref)
        note_last = note_of(first + CHUNK - 1, lens_ref)
        keep = jnp.where(note_before == note_last, 1.0, 0.0)
        note = note_of(first + rows_iota((CHUNK, LANES)), lens_ref)
        linked = note_of(first + row, lens_ref) == note_of(first + col, lens_ref)
        b_parts = (hi_ref[:, :N], lo_ref[:, :N])
        c_parts = (hi_ref[:, N:], lo_ref[:, N:])
        return keep, note == note_before, note == note_last, linked, b_parts, c_parts

    def walk(ref, left, turn, x_refs, keep, place, over):
        held = ref[:, over]
        held_parts = split(held)
        x_parts = (x_refs[0][:, over], x_refs[1][:, over])
        right = below(held_parts, x_parts)
        fresh = dot(turn, stack(x_parts[0], x_parts[0], x_parts[1]))
        moved = (held * keep + fresh) * kappa_ref[pl.ds(place, 1), over]
        ref[:, over] = moved * kappa_ref[pl.ds(chunks + place, 1), over]
        return dot3(left, right), right, held_parts

    rows_f = pl.ds(pl.multiple_of(here * CHUNK, CHUNK), CHUNK)
    rows_b = pl.ds(pl.multiple_of(there * CHUNK, CHUNK), CHUNK)
    f_keep, f_enters, f_leaves, f_linked, fb, fc = setting(here, f_hi, f_lo)
    b_keep, b_enters, b_leaves, b_linked, bb, bc = setting(there, b_hi, b_lo)
    f_scores = jnp.where(f_linked & (col < row), dot3(fc, fb, NT), 0.0)
    b_scores = jnp.where(b_linked & (row < col), dot3(bb, bc, NT), 0.0)
    f_left = beside(pick(f_enters, fc), split(f_scores))
    b_left = beside(pick(b_leaves, bb), split(b_scores))
    f_turn, b_turn = turned(pick(f_leaves, fb)), turned(pick(b_enters, bc))
    own = jnp.sum(whole_of(bb) * whole_of(bc), axis=1, keepdims=True)
    wide = min(2 * LANES, channels)
    inner = outer = 0.0
    for first in range(0, channels, wide):
        over = slice(first, first + wide)
        y, right, _ = walk(state, f_left, f_turn, (fx_h, fx_l), f_keep, here, over)
        inner = inner + dot3((fg_h[:, over], fg_l[:, over]), right, NT)
        product[0:CHUNK, over], product[CHUNK : 2 * CHUNK, over] = split(
            whole_of((fg_h[:, over], fg_l[:, over])) * y
        )
        before = jnp.maximum(there - 1, 0)
        dx, _, a_parts = walk(adjoint, b_left, b_turn, (bg_h, bg_l), b_keep, before, over)
        outer = outer + dot3((bx_h[:, over], bx_l[:, over]), a_parts, NT)
        dx_ref[:, over] = dx + own * whole_of((bg_h[:, over], bg_l[:, over]))
        product[2 * CHUNK : 3 * CHUNK, over], product[3 * CHUNK :, over] = split(
            whole_of((bx_h[:, over], bx_l[:, over])) * dx
        )
    d_scores = split(jnp.where(f_linked & (col <= row), inner[:, N:], 0.0))
    for_c = jnp.where(f_enters, inner[:, :N], 0.0) + dot3(d_scores, fb)
    for_b = dot3_tn(d_scores, fc)
    dbc_ref[rows_f, :] += jnp.concatenate([for_b, for_c], axis=1)
    dbc_ref[rows_b, :N] += jnp.where(b_leaves, outer, 0.0)
    rates = dot(product[...], summer[...])
    rate_ref[rows_f, :] += rates[:CHUNK] + rates[CHUNK : 2 * CHUNK]
    rate_ref[rows_b, :] -= rates[2 * CHUNK : 3 * CHUNK] + rates[3 * CHUNK :]


def joined(messages):
    total = jnp.zeros((N, messages[0].shape[1]), f32)
    for message in reversed(messages):
        total = message[0:N, :] + message[N : N + 1, :] * total
    return total


def pull(high, low, both):
    most = dot(high, both[...], NT)
    return most[:, :N] + most[:, N:] + dot(low, both[0:N, :], NT)


def push(high, low, both, over=slice(None)):
    first = both[0:N, over]
    return dot(jnp.concatenate([high, low, high], axis=1), stack(first, first, both[N:, over]))


def entering_kernel(start_ref, *refs, count, heads, tokens):
    messages = refs[: count - 1]
    place = start_ref[0]
    forward = [
        jnp.where(place >= lag * tokens, messages[lag - 1][...], 0.0) for lag in range(1, count)
    ]
    backward = [
        jnp.where(place + lag * tokens < count * tokens, messages[count - 1 - lag][...], 0.0)
        for lag in range(1, count)
    ]
    (
        own_ref, gh_ref, gl_ref, xh_ref, xl_ref, hi_ref, lo_ref, scale_ref, dx_ref, dbc_ref,
        slope_ref, slope_bc_ref, s2_ref, a2_ref, end_ref, head_ref,
    ) = refs[count - 1 :]
    channels = gh_ref.shape[1]
    state, adjoint = joined(forward), joined(backward)
    s2_ref[0:N, :], s2_ref[N:, :] = split(state)
    a2_ref[0:N, :], a2_ref[N:, :] = split(adjoint)
    last = own_ref[0:N, :] + own_ref[N : N + 1, :] * state
    end_ref[...] = jnp.broadcast_to(jnp.sum(last * adjoint, axis=0, keepdims=True), end_ref.shape)
    for_c = pull(gh_ref[...], gl_ref[...], s2_ref)
    for_b = pull(xh_ref[...], xl_ref[...], a2_ref)
    shared = (dbc_ref[...] + jnp.concatenate([for_b, for_c], axis=1)) * slope_bc_ref[...]
    scale = scale_ref[...]
    dx = dx_ref[...] * dot(scale, expander(heads, channels, 1))
    dx = dx + push(hi_ref[:, :N], lo_ref[:, :N], a2_ref) * dot(scale, expander(heads, channels, 3))
    head_ref[:, :channels] = (dx * slope_ref[...])[0:8, :]
    head_ref[:, channels:] = shared[0:8, :]


def shared_kernel(gh_ref, gl_ref, xh_ref, xl_ref, dbc_ref, slope_ref, s2_ref, a2_ref, out_ref):
    for_c = pull(gh_ref[...], gl_ref[...], s2_ref)
    for_b = pull(xh_ref[...], xl_ref[...], a2_ref)
    out_ref[...] = (dbc_ref[...] + jnp.concatenate([for_b, for_c], axis=1)) * slope_ref[...]


def arrange_kernel(
    lens_ref, start_ref, side_ref, shared_ref, halo_ref, taps_ref, keep_ref, give_ref, ext, total, *, sharers
):
    tokens = shared_ref.shape[0]
    ext[0:tokens, :] = shared_ref[...]
    ext[tokens:, :] = halo_ref[:, -2 * N :]
    size = tokens // sharers
    high = min(size, 64)
    odd = side_ref[0] == 1
    for block in range(sharers):
        for part in range(0, size, high):
            first = block * size + part

            def emit(over, value, at=slice(first, first + high)):
                total[at, over] = value

            conv_rows(ext, taps_ref, first, high, 2 * N, start_ref[0] + first, 1, lens_ref, emit)
    for pair in range(sharers // 2):
        even, uneven = (total[(2 * pair + i) * size : (2 * pair + i + 1) * size, :] for i in range(2))
        at = slice(pair * size, (pair + 1) * size)
        keep_ref[at, :] = jnp.where(odd, uneven, even)
        give_ref[at, :] = jnp.where(odd, even, uneven)


def final_kernel(
    lens_ref, start_ref, gh_ref, gl_ref, xh_ref, xl_ref, hi_ref, lo_ref, scale_ref,
    dx_ref, slope_ref, rate_ref, s2_ref, a2_ref, taps_ref, tail_ref, from_ref,
    *refs, heads, first_block, last
):
    out_ref, log_ref, head_ref, carry, spread, spread_q, summer, ext = refs[-13:-5]
    product, y_tile, dx_tile, near, leave = refs[-5:]
    step = pl.program_id(0)
    rows, channels = gh_ref.shape

    @pl.when(step == 0)
    def _():
        spread[...] = expander(heads, channels, 3)
        spread_q[...] = expander(heads, channels, 1)
        summer[...] = head_summer(channels)
        ext[rows:, :] = tail_ref[:, :channels]
        carry[...] = jnp.zeros_like(carry) if last else from_ref[...]

    @pl.when(step > 0)
    def _():
        ext[rows:, :] = ext[0:8, :]

    scale = scale_ref[...]
    wide = min(2 * LANES, channels)
    for c in range(0, channels, wide):
        whole = slice(c, c + wide)
        y_tile[...] = push(hi_ref[:, N:], lo_ref[:, N:], s2_ref, whole)
        dx_tile[...] = push(hi_ref[:, :N], lo_ref[:, :N], a2_ref, whole)
        near[...] = dot(scale, spread_q[:, whole])
        leave[...] = dot(scale, spread[:, whole])
        for at, inside in tiles(rows, wide):
            over = slice(c + inside.start, c + inside.stop)
            dx = dx_tile[at, inside]
            rate = whole_of((gh_ref[at, over], gl_ref[at, over])) * y_tile[at, inside]
            rate = rate - whole_of((xh_ref[at, over], xl_ref[at, over])) * dx
            product[at, over], product[rows + at.start : rows + at.stop, over] = split(rate)
            grad = dx_ref[at, over] * near[at, inside] + dx * leave[at, inside]
            ext[at, over] = grad * slope_ref[at, over]
    rates = dot(product[...], summer[...])
    rates = rate_ref[...] + rates[:rows] + rates[rows:]
    if last:
        end_row = (rows_iota((rows, LANES)) == rows - 1) & (step == 0)
        beyond = exact(thirds(from_ref[...]), summer[...])[0:1, :]
        rates = rates + jnp.where(end_row, beyond, 0.0)
    later = rows_iota((rows, rows)) >= cols_iota((rows, rows))
    ones = jnp.ones((rows, LANES), f32)
    marks = jnp.concatenate([jnp.where(later, 1.0, 0.0), ones], axis=1).astype(bf16)
    sums = exact(thirds(rates), marks, TN)
    log = sums[:, :rows] + widen(carry[...], rows)
    log_ref[...] = log[0:heads, :]
    carry[...] += sums[:, rows:]
    first = start_ref[0] + (first_block - step) * rows
    for r in range(0, rows, 64):

        def emit(over, value, at=slice(r, r + 64)):
            out_ref[at, over] = value

        conv_rows(ext, taps_ref, r, 64, channels, first + r, 1, lens_ref, emit)

    @pl.when(step == pl.num_programs(0) - 1)
    def _():
        head_ref[...] = ext[0:8, :]


def shifted(value, axis, steps):
    count = lax.axis_size(axis)
    initial, last = (max(0, -steps), min(count, count - steps))
    return lax.ppermute(value, axis, [(source, source + steps) for source in range(initial, last)])


def head_scatter(keep, give):
    count = lax.axis_size("head")
    mine = lax.axis_index("head")
    swap = lambda value, bit: lax.ppermute(value, "head", [(i, i ^ bit) for i in range(count)])
    value = keep + swap(give, 1)
    size = 2 * value.shape[0] // count
    value = value.reshape(count // 2, size, value.shape[1])
    bit = 2
    while bit < count:
        pairs = value.reshape(value.shape[0] // 2, 2, size, value.shape[2])
        side = (mine // bit) % 2
        kept = lax.dynamic_index_in_dim(pairs, side, 1, keepdims=False)
        given = lax.dynamic_index_in_dim(pairs, 1 - side, 1, keepdims=False)
        value = kept + swap(given, bit)
        bit *= 2
    return value.reshape(size, value.shape[2])


def local(pre_x, pre_bc, conv_x, conv_bc, log_decay, lengths, grad_out):
    tokens, channels = pre_x.shape
    heads = log_decay.shape[0]
    count = lax.axis_size("seq")
    sharers = lax.axis_size("head")
    chunks = tokens // CHUNK
    big = 256
    steps = tokens // big
    width = 2 * LANES
    start = (lax.axis_index("seq") * tokens).astype(jnp.int32).reshape(1)
    side = (lax.axis_index("head") % 2).astype(jnp.int32).reshape(1)
    halo = shifted(jnp.concatenate([pre_x[-16:], pre_bc[-16:]], axis=1), "seq", 1)
    shape = jax.ShapeDtypeStruct
    smem = pl.BlockSpec(memory_space=pltpu.SMEM)
    vmem = pl.BlockSpec(memory_space=pltpu.VMEM)
    params = pltpu.CompilerParams(vmem_limit_bytes=VMEM_LIMIT)
    by_rows = lambda rows, cols: pl.BlockSpec((rows, cols), lambda i: (i, 0))
    whole = lambda rows, cols: pl.BlockSpec((rows, cols), lambda *i: (0, 0))
    wide = tokens * channels
    cost = lambda work: pl.CostEstimate(flops=wide * work, bytes_accessed=wide * 16, transcendentals=0)
    rows_f32, rows_bf16 = shape((tokens, channels), f32), shape((tokens, channels), bf16)
    bc_f32, bc_bf16 = shape((tokens, 2 * N), f32), shape((tokens, 2 * N), bf16)

    scale, kappa, through = pl.pallas_call(
        scales_kernel,
        out_shape=(
            shape((tokens, width), bf16), shape((2 * chunks, channels), f32), shape((8, channels), f32),
        ),
        in_specs=[smem, smem, vmem],
        out_specs=(vmem,) * 3,
        scratch_shapes=[pltpu.VMEM((LANES, tokens), f32)],
        compiler_params=params,
        cost_estimate=cost(1000),
    )(lengths, start, log_decay)

    spread = pltpu.VMEM((width, channels), bf16)
    block = pltpu.VMEM((big, channels), f32)
    hi, lo, slope_bc, r_high, r_low, g_high, g_low, send_adjoint = pl.pallas_call(
        functools.partial(adjoint_kernel, heads=heads),
        grid=(steps,),
        out_shape=(bc_bf16, bc_bf16, bc_f32) + (rows_bf16,) * 4 + (shape((N + 8, channels), f32),),
        in_specs=[
            smem, smem, by_rows(big, channels), by_rows(big, width), by_rows(big, 2 * N),
            whole(16, channels + 2 * N), whole(K, 2 * N), whole(8, channels),
        ],
        out_specs=(by_rows(big, 2 * N),) * 3 + (by_rows(big, channels),) * 4 + (whole(N + 8, channels),),
        scratch_shapes=[spread, spread, block, block, pltpu.VMEM((big + 8, 2 * N), f32)],
        compiler_params=params,
        cost_estimate=cost(1000),
    )(lengths, start, grad_out, scale, pre_bc, halo, conv_bc, through)

    slope_x, q_high, q_low, x_high, x_low, own_state, *messages = pl.pallas_call(
        functools.partial(state_kernel, heads=heads, count=count),
        grid=(steps,),
        out_shape=(rows_f32,) + (rows_bf16,) * 4 + (shape((N + 8, channels), f32),) * count,
        in_specs=[
            smem, smem, by_rows(big, channels), whole(16, channels + 2 * N), whole(K, channels),
            by_rows(big, width), by_rows(big, 2 * N), by_rows(big, 2 * N), whole(8, channels),
            whole(N + 8, channels),
        ],
        out_specs=(by_rows(big, channels),) * 5 + (whole(N + 8, channels),) * count,
        scratch_shapes=[spread, spread, block, block, pltpu.VMEM((big + 8, channels), f32)],
        compiler_params=params,
        cost_estimate=cost(1000),
    )(lengths, start, pre_x, halo, conv_x, scale, hi, lo, through, send_adjoint)
    received = [
        lax.ppermute(message, "seq", [(i, (i + lag) % count) for i in range(count)])
        for lag, message in enumerate(messages, 1)
    ]

    from_end = lambda rows, cols: pl.BlockSpec((rows, cols), lambda i: (chunks - 1 - i, 0))
    both_ways = [
        place(CHUNK, size)
        for place in (by_rows, from_end)
        for size in (channels, channels, channels, channels, 2 * N, 2 * N)
    ]
    dx, dbc, rate = pl.pallas_call(
        local_kernel,
        grid=(chunks,),
        out_shape=(rows_f32, bc_f32, shape((tokens, LANES), f32)),
        in_specs=[smem, smem, whole(2 * chunks, channels)] + both_ways,
        out_specs=(from_end(CHUNK, channels), whole(tokens, 2 * N), whole(tokens, LANES)),
        scratch_shapes=[
            pltpu.VMEM((N, channels), f32), pltpu.VMEM((N, channels), f32),
            pltpu.VMEM((channels, LANES), bf16),
        ]
        + [pltpu.VMEM((4 * CHUNK, channels), bf16)],
        compiler_params=params,
        cost_estimate=cost(8000),
    )(lengths, start, kappa, *([q_high, q_low, r_high, r_low, hi, lo] * 2))

    message = whole(N + 8, channels)
    s2, a2, end, head = pl.pallas_call(
        functools.partial(entering_kernel, count=count, heads=heads, tokens=tokens),
        grid=(1,),
        out_shape=(
            shape((2 * N, channels), bf16), shape((2 * N, channels), bf16), shape((8, channels), f32),
            shape((8, channels + 2 * N), f32),
        ),
        in_specs=[smem]
        + [message] * count
        + [whole(16, channels)] * 4
        + [whole(16, 2 * N)] * 2
        + [whole(16, width), whole(16, channels), whole(16, 2 * N), whole(16, channels), whole(16, 2 * N)],
        out_specs=(
            whole(2 * N, channels), whole(2 * N, channels), whole(8, channels),
            whole(8, channels + 2 * N),
        ),
        compiler_params=params,
        cost_estimate=cost(200),
    )(
        start, *received, own_state, g_high, g_low, x_high, x_low, hi, lo, scale, dx, dbc,
        slope_x, slope_bc,
    )
    after = shifted(head, "seq", -1)

    shared = pl.pallas_call(
        shared_kernel,
        grid=(steps,),
        out_shape=bc_f32,
        in_specs=[by_rows(big, channels)] * 4
        + [by_rows(big, 2 * N)] * 2
        + [whole(2 * N, channels)] * 2,
        out_specs=by_rows(big, 2 * N),
        compiler_params=params,
        cost_estimate=cost(1500),
    )(g_high, g_low, x_high, x_low, dbc, slope_bc, s2, a2)

    half = shape((tokens // 2, 2 * N), f32)
    keep, give = pl.pallas_call(
        functools.partial(arrange_kernel, sharers=sharers),
        out_shape=(half, half),
        in_specs=[smem, smem, smem, vmem, vmem, vmem],
        out_specs=(vmem, vmem),
        scratch_shapes=[pltpu.VMEM((tokens + 8, 2 * N), f32), pltpu.VMEM((tokens, 2 * N), f32)],
        compiler_params=params,
    )(lengths, start, side, shared, after, conv_bc)
    grad_pre_bc = head_scatter(keep, give)

    part = steps // 2
    tail, carry = after, end
    done = ()
    for first_block in (steps - 1, steps - 1 - part):
        back = lambda rows, cols, top=first_block: pl.BlockSpec((rows, cols), lambda i: (top - i, 0))
        grad_pre_x, grad_log, tail, carry = pl.pallas_call(
            functools.partial(final_kernel, heads=heads, first_block=first_block, last=not done),
            grid=(part,),
            out_shape=(
                rows_f32, shape((heads, tokens), f32), shape((8, channels), f32),
                shape((LANES, LANES), f32),
            ),
            in_specs=[smem, smem]
            + [back(big, channels)] * 4
            + [back(big, 2 * N)] * 2
            + [back(big, width)]
            + [back(big, channels)] * 2
            + [
                back(big, LANES), whole(2 * N, channels), whole(2 * N, channels),
                whole(K, channels), whole(*tail.shape), whole(*carry.shape),
            ]
            + [pl.BlockSpec(memory_space=pl.ANY)] * len(done),
            out_specs=(
                back(big, channels),
                pl.BlockSpec((heads, big), lambda i, top=first_block: (0, top - i)),
                whole(8, channels), whole(LANES, LANES),
            ),
            scratch_shapes=[
                spread, spread, pltpu.VMEM((channels, LANES), bf16),
                pltpu.VMEM((big + 8, channels), f32), pltpu.VMEM((2 * big, channels), bf16),
            ]
            + [pltpu.VMEM((big, min(2 * LANES, channels)), f32)] * 4,
            input_output_aliases={17 + i: i for i in range(len(done))},
            compiler_params=params,
            cost_estimate=cost(1500),
        )(
            lengths, start, g_high, g_low, x_high, x_low, hi, lo, scale, dx, slope_x, rate, s2, a2,
            conv_x, tail, carry, *done,
        )
        done = (grad_pre_x, grad_log)
    return (grad_pre_x, grad_pre_bc, grad_log)


def solution(mesh):
    placed = (
        P("seq", "head"),
        P("seq", None),
        P(None, "head"),
        P(),
        P("head", "seq"),
        P(),
        P("seq", "head"),
    )
    return jax.shard_map(
        local,
        mesh=mesh,
        in_specs=placed,
        out_specs=(P("seq", "head"), P(("seq", "head"), None), P("head", "seq")),
        check_vma=False,
    )
```

profile of v0, /device:TPU:0, one launch (start us, length us, event | category | flops | bytes accessed | tf_op | source)
XLA Modules:
  0.0 107.8 jit_solution(15060437097288691560)
XLA Ops:
  0.6 0.8 slice.6
  1.4 0.7 slice.7
  2.1 4.8 %collective-permute-start = (bf16[16,1280]{1,0:T(8,128)(2,1)S(1)}, bf16[16,1280]{1,0:T(8,128)(2,1)S(1)}, u32[]{:S(2)}, u32[]{:S(2)}) collective-permute-start(bf16[16,1280]{1,0:T(8,128)(2,1)S(1)} %pad_maximum_fusion), channel_id=1, source_target_pairs={{0,8},{8,16},{16,24},{1,9},{9,17},{17,25},{2,10},{10,18},{18,26},{... | collective-permute-start | bytes 122888 | tf_op jit(solution)/shard_map/ppermute | solution.py:510
  6.9 4.4 %shard_map.94 = (bf16[1024,256]{1,0:T(8,128)(2,1)}, f32[32,1024]{1,0:T(8,128)}, f32[8,1024]{1,0:T(8,128)}) custom-call(s32[4]{0:T(128)} %lens_ref.13, s32[1]{0:T(128)} %bitcast.start_ref, f32[16,1024]{1,0:T(8,128)} %log_ref.1), custom_call_target="tpu_custom_call" | custom-call | flops 1048576000 | bytes 16777216 | tf_op jit(solution)/shard_map/pallas_call | solution.py:554
  11.3 0.0 collective-permute-done.halo_ref
  11.3 0.0 copy-start.4
  11.3 0.6 copy-done.4
  11.9 9.5 %shard_map.95 = (bf16[1024,256]{1,0:T(8,128)(2,1)}, bf16[1024,256]{1,0:T(8,128)(2,1)}, f32[1024,256]{1,0:T(8,128)}, bf16[1024,1024]{1,0:T(8,128)(2,1)}, bf16[102...) custom-call(s32[4]{0:T(128)} %lens_ref.13, ...), custom_call_target="tpu_custom_call" | custom-call | flops 1048576000 | bytes 16777216 | tf_op jit(solution)/shard_map/pallas_call | solution.py:568
  21.4 13.3 %shard_map.96 = (f32[1024,1024]{1,0:T(8,128)}, bf16[1024,1024]{1,0:T(8,128)(2,1)}, bf16[1024,1024]{1,0:T(8,128)(2,1)}, bf16[1024,1024]{1,0:T(8,128)(2,1)}, bf16[...) custom-call(s32[4]{0:T(128)} %lens_ref.13, ...), custom_call_target="tpu_custom_call" | custom-call | flops 1048576000 | bytes 16777216 | tf_op jit(solution)/shard_map/pallas_call | solution.py:582
  34.7 1.5 %collective-permute-start.1 = (f32[136,1024]{1,0:T(8,128)}, f32[136,1024]{1,0:T(8,128)S(1)}, u32[]{:S(2)}, u32[]{:S(2)}) collective-permute-start(f32[136,1024]{1,0:T(8,128)} %get-tuple-element.55), channel_id=1, source_target_pairs={{0,8},{8,16},{16,24},{24,0},{1,9},{9,17},{17,25},{25,1},{2,10},{10... | collective-permute-start | bytes 1671176 | tf_op jit(solution)/shard_map/ppermute | solution.py:597
  36.3 0.1 collective-permute-start.2
  36.4 2.8 %collective-permute-start.3 = (f32[136,1024]{1,0:T(8,128)}, f32[136,1024]{1,0:T(8,128)S(1)}, u32[]{:S(2)}, u32[]{:S(2)}) collective-permute-start(f32[136,1024]{1,0:T(8,128)} %get-tuple-element.57), channel_id=1, source_target_pairs={{0,24},{8,0},{16,8},{24,16},{1,25},{9,1},{17,9},{25,17},{2,26},{10... | collective-permute-start | bytes 1671176 | tf_op jit(solution)/shard_map/ppermute | solution.py:597
  39.2 24.2 %shard_map.97 = (f32[1024,1024]{1,0:T(8,128)}, f32[1024,256]{1,0:T(8,128)}, f32[1024,128]{1,0:T(8,128)}) custom-call(s32[4]{0:T(128)} %lens_ref.13, s32[1]{0:T(128)} %bitcast.start_ref, f32[32,1024]{1,0:T(8,128)} %get-tuple-element.47.kappa_ref, bf16[1024,1024]{1,0:T(8,128)(2,1)} %get-tuple-element.48.fx_h.bx_h, ...), custom_call_target="tpu_custom_call" | custom-call | flops 8388608000 | bytes 16777216 | tf_op jit(solution)/shard_map/pallas_call | solution.py:607
  63.5 0.0 collective-permute-done.1.refs_0_
  63.5 0.0 copy-start
  63.5 0.0 collective-permute-done.2.refs_1_
  63.5 0.0 copy-start.1
  63.5 0.0 collective-permute-done.3.refs_2_
  63.5 0.0 copy-start.2
  63.5 0.8 copy-done
  64.3 0.2 copy-done.1
  64.5 0.2 copy-done.2
  64.7 3.2 %shard_map.98 = (bf16[256,1024]{1,0:T(8,128)(2,1)}, bf16[256,1024]{1,0:T(8,128)(2,1)}, f32[8,1024]{1,0:T(8,128)}, f32[8,1280]{1,0:T(8,128)}) custom-call(s32[1]{0:T(128)} %bitcast.start_ref, f32[136,1024]{1,0:T(8,128)} %copy-done, f32[136,1024]{1,0:T(8,128)} %copy-done.1, f32[136,1024]{1,0:T(8,128)} %copy-done.2, f32[136,1024]{1,0:T(8,128)} %get-tuple-element.58.refs_3_, ...), custom_call_target="tpu_custom_call" | custom-call | flops 209715200 | bytes 16777216 | tf_op jit(solution)/shard_map/pallas_call | solution.py:623
  67.9 1.5 %collective-permute-start.4 = (f32[8,1280]{1,0:T(8,128)}, f32[8,1280]{1,0:T(8,128)S(1)}, u32[]{:S(2)}, u32[]{:S(2)}) collective-permute-start(f32[8,1280]{1,0:T(8,128)} %get-tuple-element.63), channel_id=1, source_target_pairs={{8,0},{16,8},{24,16},{9,1},{17,9},{25,17},{10,2},{18,10},{26,18},{... | collective-permute-start | bytes 122888 | tf_op jit(solution)/shard_map/ppermute | solution.py:510
  69.3 7.3 %shard_map.101.shared_ref = f32[1024,256]{1,0:T(8,128)} custom-call(bf16[1024,1024]{1,0:T(8,128)(2,1)} %get-tuple-element.40.refs_4_.gh_ref, bf16[1024,1024]{1,0:T(8,128)(2,1)} %get-tuple-element.41.refs_5_.gl_ref, bf16[1024,1024]{1,0:T(8,128)(2,1)} %get-tuple-element.45.refs_6_.xh_ref, bf16[1024,1024]{1,0:T(8,128)(2,1)} %get-tuple-element.46.refs_7_.xl_ref, ...), custom_call_target="tpu_custom_call" | custom-call | flops 1572864000 | bytes 16777216 | tf_op jit(solution)/shard_map/pallas_call | solution.py:647
  76.6 0.0 collective-permute-done.4.tail_ref.halo_ref
  76.6 0.0 copy-start.3
  76.6 0.6 copy-done.3
  77.2 3.2 %shard_map.102 = (f32[512,256]{1,0:T(8,128)}, f32[512,256]{1,0:T(8,128)}) custom-call(s32[4]{0:T(128)} %lens_ref.13, s32[1]{0:T(128)} %bitcast.start_ref, s32[1]{0:T(128)} %bitcast.1.side_ref, f32[1024,256]{1,0:T(8,128)} %shard_map.101.shared_ref, f32[8,1280]{1,0:T(8,128)} %copy-done.3, f32[4,256]{1,0:T(4,128)} %taps_ref.9), custom_call_target="tpu_custom_call" | custom-call | tf_op jit(solution)/shard_map/pallas_call | solution.py:660
  80.4 0.0 collective-permute-start.5
  80.4 2.1 %collective-permute-done.5 = f32[512,256]{1,0:T(8,128)S(1)} collective-permute-done((f32[512,256]{1,0:T(8,128)}, f32[512,256]{1,0:T(8,128)S(1)}, u32[]{:S(2)}, u32[]{:S(2)}) %collective-permute-start.5) | collective-permute-done | bytes 524320 | tf_op jit(solution)/shard_map/ppermute | solution.py:516
  82.6 1.1 %add.38 = f32[512,256]{1,0:T(8,128)S(1)} add(f32[512,256]{1,0:T(8,128)} %get-tuple-element.70, f32[512,256]{1,0:T(8,128)S(1)} %collective-permute-done.5) | non-fusion elementwise | flops 131072 | bytes 1572864 | tf_op jit(solution)/shard_map/add | solution.py:517
  83.7 1.6 %collective-permute-start.6 = (f32[2,128,256]{2,1,0:T(8,128)S(1)}, f32[2,128,256]{2,1,0:T(8,128)S(1)}, u32[]{:S(2)}, u32[]{:S(2)}) collective-permute-start(f32[2,128,256]{2,1,0:T(8,128)S(1)} %dynamic-slice_bitcast_fusion), channel_id=1, source_target_pairs={{0,2},{1,3},{2,0},{3,1},{4,6},{5,7},{6,4},{7,5},{8,10},{9,11},{10,... | collective-permute-start | bytes 786440 | tf_op jit(solution)/shard_map/ppermute | solution.py:516
  85.3 9.6 %shard_map.99 = (f32[1024,1024]{1,0:T(8,128)}, f32[16,1024]{1,0:T(8,128)}, f32[8,1024]{1,0:T(8,128)}, f32[128,128]{1,0:T(8,128)}) custom-call(s32[4]{0:T(128)} %lens_ref.13, s32[1]{0:T(128)} %bitcast.start_ref, bf16[1024,1024]{1,0:T(8,128)(2,1)} %get-tuple-element.40.refs_4_.gh_ref, bf16[1024,1024]{1,0:T(8,128)(2,1)} %get-tuple-element.41.refs_5_.gl_ref, ...), custom_call_target="tpu_custom_call" | custom-call | flops 1572864000 | bytes 16777216 | tf_op jit(solution)/shard_map/pallas_call | solution.py:675
  94.9 0.0 collective-permute-done.6
  95.0 2.7 %collective-permute-start.7 = (f32[1,128,256]{2,1,0:T(8,128)S(1)}, f32[1,128,256]{2,1,0:T(8,128)S(1)}, u32[]{:S(2)}, u32[]{:S(2)}) collective-permute-start(f32[1,128,256]{2,1,0:T(8,128)S(1)} %constant_dynamic-slice_fusion), channel_id=1, source_target_pairs={{0,4},{1,5},{2,6},{3,7},{4,0},{5,1},{6,2},{7,3},{8,12},{9,13},{10,... | collective-permute-start | bytes 393224 | tf_op jit(solution)/shard_map/ppermute | solution.py:516
  97.7 9.5 %shard_map.100 = (f32[1024,1024]{1,0:T(8,128)}, f32[16,1024]{1,0:T(8,128)}, f32[8,1024]{1,0:T(8,128)}, f32[128,128]{1,0:T(8,128)}) custom-call(s32[4]{0:T(128)} %lens_ref.13, s32[1]{0:T(128)} %bitcast.start_ref, bf16[1024,1024]{1,0:T(8,128)(2,1)} %get-tuple-element.40.refs_4_.gh_ref, ...), custom_call_target="tpu_custom_call", output_to_operand_aliasing={{0}: (17, {}), {1}: (18, {})} | custom-call | flops 1572864000 | bytes 16777216 | tf_op jit(solution)/shard_map/pallas_call | solution.py:675
  107.2 0.0 collective-permute-done.7
  107.2 0.7 add_bitcast_fusion
  (4 shorter events, 0.1 us)
Async XLA Ops:
  2.1 9.2 %collective-permute-start = (bf16[16,1280]{1,0:T(8,128)(2,1)S(1)}, bf16[16,1280]{1,0:T(8,128)(2,1)S(1)}, u32[]{:S(2)}, u32[]{:S(2)}) collective-permute-start(bf16[16,1280]{1,0:T(8,128)(2,1)S(1)} %pad_maximum_fusion), channel_id=1, source_target_pairs={{0,8},{8,16},{16,24},{1,9},{9,17},{17,25},{2,10},{10,18},{18,26},{... | collective-permute-start | bytes 122888 | tf_op jit(solution)/shard_map/ppermute | solution.py:510
  11.3 0.6 copy-start.4
  34.7 28.7 %collective-permute-start.1 = (f32[136,1024]{1,0:T(8,128)}, f32[136,1024]{1,0:T(8,128)S(1)}, u32[]{:S(2)}, u32[]{:S(2)}) collective-permute-start(f32[136,1024]{1,0:T(8,128)} %get-tuple-element.55), channel_id=1, source_target_pairs={{0,8},{8,16},{16,24},{24,0},{1,9},{9,17},{17,25},{25,1},{2,10},{10... | collective-permute-start | bytes 1671176 | tf_op jit(solution)/shard_map/ppermute | solution.py:597
  36.3 27.2 %collective-permute-start.2 = (f32[136,1024]{1,0:T(8,128)}, f32[136,1024]{1,0:T(8,128)S(1)}, u32[]{:S(2)}, u32[]{:S(2)}) collective-permute-start(f32[136,1024]{1,0:T(8,128)} %get-tuple-element.56), channel_id=1, source_target_pairs={{0,16},{8,24},{16,0},{24,8},{1,17},{9,25},{17,1},{25,9},{2,18},{10... | collective-permute-start | bytes 1671176 | tf_op jit(solution)/shard_map/ppermute | solution.py:597
  36.4 27.1 %collective-permute-start.3 = (f32[136,1024]{1,0:T(8,128)}, f32[136,1024]{1,0:T(8,128)S(1)}, u32[]{:S(2)}, u32[]{:S(2)}) collective-permute-start(f32[136,1024]{1,0:T(8,128)} %get-tuple-element.57), channel_id=1, source_target_pairs={{0,24},{8,0},{16,8},{24,16},{1,25},{9,1},{17,9},{25,17},{2,26},{10... | collective-permute-start | bytes 1671176 | tf_op jit(solution)/shard_map/ppermute | solution.py:597
  63.5 0.8 copy-start
  63.5 1.0 copy-start.1
  63.5 1.1 %copy-start.2 = (f32[136,1024]{1,0:T(8,128)}, f32[136,1024]{1,0:T(8,128)S(1)}, u32[]{:S(2)}) copy-start(f32[136,1024]{1,0:T(8,128)S(1)} %collective-permute-done.3.refs_2_) | copy-start | bytes 1671172
  67.9 8.8 %collective-permute-start.4 = (f32[8,1280]{1,0:T(8,128)}, f32[8,1280]{1,0:T(8,128)S(1)}, u32[]{:S(2)}, u32[]{:S(2)}) collective-permute-start(f32[8,1280]{1,0:T(8,128)} %get-tuple-element.63), channel_id=1, source_target_pairs={{8,0},{16,8},{24,16},{9,1},{17,9},{25,17},{10,2},{18,10},{26,18},{... | collective-permute-start | bytes 122888 | tf_op jit(solution)/shard_map/ppermute | solution.py:510
  76.6 0.6 copy-start.3
  80.4 2.1 %collective-permute-start.5 = (f32[512,256]{1,0:T(8,128)}, f32[512,256]{1,0:T(8,128)S(1)}, u32[]{:S(2)}, u32[]{:S(2)}) collective-permute-start(f32[512,256]{1,0:T(8,128)} %get-tuple-element.71), channel_id=1, source_target_pairs={{0,1},{1,0},{2,3},{3,2},{4,5},{5,4},{6,7},{7,6},{8,9},{9,8},{10,11... | collective-permute-start | bytes 1572872 | tf_op jit(solution)/shard_map/ppermute | solution.py:516
  83.7 11.2 %collective-permute-start.6 = (f32[2,128,256]{2,1,0:T(8,128)S(1)}, f32[2,128,256]{2,1,0:T(8,128)S(1)}, u32[]{:S(2)}, u32[]{:S(2)}) collective-permute-start(f32[2,128,256]{2,1,0:T(8,128)S(1)} %dynamic-slice_bitcast_fusion), channel_id=1, source_target_pairs={{0,2},{1,3},{2,0},{3,1},{4,6},{5,7},{6,4},{7,5},{8,10},{9,11},{10,... | collective-permute-start | bytes 786440 | tf_op jit(solution)/shard_map/ppermute | solution.py:516
  95.0 12.2 %collective-permute-start.7 = (f32[1,128,256]{2,1,0:T(8,128)S(1)}, f32[1,128,256]{2,1,0:T(8,128)S(1)}, u32[]{:S(2)}, u32[]{:S(2)}) collective-permute-start(f32[1,128,256]{2,1,0:T(8,128)S(1)} %constant_dynamic-slice_fusion), channel_id=1, source_target_pairs={{0,4},{1,5},{2,6},{3,7},{4,0},{5,1},{6,2},{7,3},{8,12},{9,13},{10,... | collective-permute-start | bytes 393224 | tf_op jit(solution)/shard_map/ppermute | solution.py:516
where the time goes:
time: 109 us; the launch traced here: 108 us
  Pallas kernels  84.1 us (77%)
  starting transfers between devices  15.1 us (14%)
  local copies, waits for them, and re-layouts  3.87 us (4%)
  waiting for transfers between devices  2.14 us (2%)
  other arithmetic  1.83 us (2%)
    pallas_call x1, Pallas kernels, local(): pl.pallas_call(local_kernel, grid=(chunks,), out_shape=(rows_f32, bc_f32,...  24.2 us
    pallas_call x2, Pallas kernels, local(): pl.pallas_call(functools.partial(final_kernel, heads=heads, first_block=f...  19.1 us
    pallas_call x1, Pallas kernels, local(): pl.pallas_call(functools.partial(state_kernel, heads=heads, count=count),...  13.3 us
    pallas_call x1, Pallas kernels, local(): pl.pallas_call(functools.partial(adjoint_kernel, heads=heads), grid=(step...  9.48 us
    pallas_call x1, Pallas kernels, local(): pl.pallas_call(shared_kernel, grid=(steps,), out_shape=bc_f32, in_specs=[...  7.29 us
    ppermute x2, starting transfers between devices, shifted(): lax.ppermute(value, axis, [(source, source + steps) for source in range(i...  6.29 us
    ppermute x3, starting transfers between devices, local(): lax.ppermute(message, 'seq', [(i, (i + lag) % count) for i in range(count)])  4.5 us
    pallas_call x1, Pallas kernels, local(): pl.pallas_call(scales_kernel, out_shape=(shape((tokens, width), bf16), sh...  4.38 us
  transfers between devices with their start and end apart: 8, of which 1 were waited for; matrix products, arithmetic and copies ran while one was open for 0% of the time, Pallas kernels for 51%

commit v1 on v0

--- a/solution.py
+++ b/solution.py
@@ -16,7 +16,7 @@
 NN = (((1,), (0,)), ((), ()))
 NT = (((1,), (1,)), ((), ()))
 TN = (((0,), (0,)), ((), ()))
-VMEM_LIMIT = 56 * 1024 * 1024
+VMEM_LIMIT = 24 * 1024 * 1024
 
 
 def split(value):
@@ -424,7 +424,7 @@
     ext[tokens:, :] = halo_ref[:, -2 * N :]
     size = tokens // sharers
     high = min(size, 64)
-    odd = side_ref[0] == 1
+    odd = side_ref[0] % 2 == 1
     for block in range(sharers):
         for part in range(0, size, high):
             first = block * size + part
@@ -510,22 +510,44 @@
     return lax.ppermute(value, axis, [(source, source + steps) for source in range(initial, last)])
 
 
-def head_scatter(keep, give):
+def merge_kernel(side_ref, kept_ref, came_ref, keep_ref, give_ref):
+    odd = side_ref[0] == 1
+    for pair in range(keep_ref.shape[0]):
+        even, uneven = (kept_ref[2 * pair + i] + came_ref[2 * pair + i] for i in range(2))
+        keep_ref[pair] = jnp.where(odd, uneven, even)
+        give_ref[pair] = jnp.where(odd, even, uneven)
+
+
+def last_kernel(kept_ref, came_ref, out_ref):
+    out_ref[...] = kept_ref[...] + came_ref[...]
+
+
+def head_scatter(keep, give, mine, params):
     count = lax.axis_size("head")
-    mine = lax.axis_index("head")
     swap = lambda value, bit: lax.ppermute(value, "head", [(i, i ^ bit) for i in range(count)])
-    value = keep + swap(give, 1)
-    size = 2 * value.shape[0] // count
-    value = value.reshape(count // 2, size, value.shape[1])
-    bit = 2
-    while bit < count:
-        pairs = value.reshape(value.shape[0] // 2, 2, size, value.shape[2])
-        side = (mine // bit) % 2
-        kept = lax.dynamic_index_in_dim(pairs, side, 1, keepdims=False)
-        given = lax.dynamic_index_in_dim(pairs, 1 - side, 1, keepdims=False)
-        value = kept + swap(given, bit)
+    size, width = 2 * keep.shape[0] // count, keep.shape[1]
+    blocks = lambda value: value.reshape(-1, size, width)
+    smem = pl.BlockSpec(memory_space=pltpu.SMEM)
+    vmem = pl.BlockSpec(memory_space=pltpu.VMEM)
+    keep, give, bit = blocks(keep), blocks(give), 1
+    while 2 * bit < count:
+        came = swap(give, bit)
         bit *= 2
-    return value.reshape(size, value.shape[2])
+        half = jax.ShapeDtypeStruct((keep.shape[0] // 2, size, width), f32)
+        keep, give = pl.pallas_call(
+            merge_kernel,
+            out_shape=(half, half),
+            in_specs=[smem, vmem, vmem],
+            out_specs=(vmem, vmem),
+            compiler_params=params,
+        )((mine // bit) % 2, keep, came)
+    return pl.pallas_call(
+        last_kernel,
+        out_shape=jax.ShapeDtypeStruct((size, width), f32),
+        in_specs=[vmem, vmem],
+        out_specs=vmem,
+        compiler_params=params,
+    )(keep[0], swap(give, bit)[0])
 
 
 def local(pre_x, pre_bc, conv_x, conv_bc, log_decay, lengths, grad_out):
@@ -538,7 +560,7 @@
     steps = tokens // big
     width = 2 * LANES
     start = (lax.axis_index("seq") * tokens).astype(jnp.int32).reshape(1)
-    side = (lax.axis_index("head") % 2).astype(jnp.int32).reshape(1)
+    mine = lax.axis_index("head").astype(jnp.int32).reshape(1)
     halo = shifted(jnp.concatenate([pre_x[-16:], pre_bc[-16:]], axis=1), "seq", 1)
     shape = jax.ShapeDtypeStruct
     smem = pl.BlockSpec(memory_space=pltpu.SMEM)
@@ -548,6 +570,9 @@
     whole = lambda rows, cols: pl.BlockSpec((rows, cols), lambda *i: (0, 0))
     wide = tokens * channels
     cost = lambda work: pl.CostEstimate(flops=wide * work, bytes_accessed=wide * 16, transcendentals=0)
+    grad_out = pltpu.with_memory_space_constraint(grad_out, pltpu.HBM)
+    pre_x = pltpu.with_memory_space_constraint(pre_x, pltpu.HBM)
+    pre_bc = pltpu.with_memory_space_constraint(pre_bc, pltpu.HBM)
     rows_f32, rows_bf16 = shape((tokens, channels), f32), shape((tokens, channels), bf16)
     bc_f32, bc_bf16 = shape((tokens, 2 * N), f32), shape((tokens, 2 * N), bf16)
 
@@ -664,8 +689,8 @@
         out_specs=(vmem, vmem),
         scratch_shapes=[pltpu.VMEM((tokens + 8, 2 * N), f32), pltpu.VMEM((tokens, 2 * N), f32)],
         compiler_params=params,
-    )(lengths, start, side, shared, after, conv_bc)
-    grad_pre_bc = head_scatter(keep, give)
+    )(lengths, start, mine, shared, after, conv_bc)
+    grad_pre_bc = head_scatter(keep, give, mine, params)
 
     part = steps // 2
     tail, carry = after, end

time: 109 us -> 87.7 us (0.80)
  Pallas kernels: 84.1 us -> 63.7 us
  waiting for transfers between devices: 2.14 us -> 4.48 us
  other arithmetic: 1.83 us -> 0.01 us
    pallas_call x2, Pallas kernels: 19.1 us -> 14.1 us  [local(): pl.pallas_call(functools.partial(final_kernel, heads=heads, first_block=f...]
    pallas_call x1, Pallas kernels: 7.29 us -> 2.95 us  [local(): pl.pallas_call(shared_kernel, grid=(steps,), out_shape=bc_f32, in_specs=[...]
    pallas_call x1, Pallas kernels: 13.3 us -> 10.2 us  [local(): pl.pallas_call(functools.partial(state_kernel, heads=heads, count=count),...]
    pallas_call x1, Pallas kernels: 24.2 us -> 21.6 us  [local(): pl.pallas_call(local_kernel, grid=(chunks,), out_shape=(rows_f32, bc_f32,...]
    pallas_call x1, Pallas kernels: 3.17 us -> 0.93 us  [local(): pl.pallas_call(functools.partial(entering_kernel, count=count, heads=head...]
    ppermute x2, waiting for transfers between devices: 0.01 us -> 1.65 us  [shifted(): lax.ppermute(value, axis, [(source, source + steps) for source in range(i...]
    pallas_call x1, Pallas kernels: 3.2 us -> 1.68 us  [local(): pl.pallas_call(functools.partial(arrange_kernel, sharers=sharers), out_sh...]
    pallas_call x1, Pallas kernels: 9.48 us -> 8.02 us  [local(): pl.pallas_call(functools.partial(adjoint_kernel, heads=heads), grid=(step...]
  transfers between devices with their start and end apart: 8 -> 8, of which waited for: 1 -> 4; matrix products, arithmetic and copies ran while one was open for 0% -> 0% of each run, Pallas kernels for 51% -> 48%
where the time goes in v1:
time: 87.7 us; the launch traced here: 87.4 us
  Pallas kernels  63.7 us (73%)
  starting transfers between devices  15.4 us (18%)
  waiting for transfers between devices  4.48 us (5%)
  local copies, waits for them, and re-layouts  2.97 us (3%)
    pallas_call x1, Pallas kernels, local(): pl.pallas_call(local_kernel, grid=(chunks,), out_shape=(rows_f32, bc_f32,...  21.6 us
    pallas_call x2, Pallas kernels, local(): pl.pallas_call(functools.partial(final_kernel, heads=heads, first_block=f...  14.1 us
    pallas_call x1, Pallas kernels, local(): pl.pallas_call(functools.partial(state_kernel, heads=heads, count=count),...  10.2 us
    pallas_call x1, Pallas kernels, local(): pl.pallas_call(functools.partial(adjoint_kernel, heads=heads), grid=(step...  8.02 us
    ppermute x2, starting transfers between devices, shifted(): lax.ppermute(value, axis, [(source, source + steps) for source in range(i...  6.13 us
    ppermute x3, starting transfers between devices, local(): lax.ppermute(message, 'seq', [(i, (i + lag) % count) for i in range(count)])  4.91 us
    ppermute x3, starting transfers between devices, head_scatter(): lax.ppermute(value, 'head', [(i, i ^ bit) for i in range(count)])  4.37 us
    pallas_call x1, Pallas kernels, local(): pl.pallas_call(scales_kernel, out_shape=(shape((tokens, width), bf16), sh...  3.35 us
  transfers between devices with their start and end apart: 8, of which 4 were waited for; matrix products, arithmetic and copies ran while one was open for 0% of the time, Pallas kernels for 48%

profile of v1, /device:TPU:0, one launch (start us, length us, event | category | flops | bytes accessed | tf_op | source)
XLA Modules:
  0.0 87.4 jit_solution(10051752671544228788)
XLA Ops:
  0.6 0.0 copy-start.2
  0.6 0.0 copy-start.3
  0.7 0.8 slice.6
  1.4 0.7 slice.7
  2.1 4.8 %collective-permute-start = (bf16[16,1280]{1,0:T(8,128)(2,1)S(1)}, bf16[16,1280]{1,0:T(8,128)(2,1)S(1)}, u32[]{:S(2)}, u32[]{:S(2)}) collective-permute-start(bf16[16,1280]{1,0:T(8,128)(2,1)S(1)} %pad_maximum_fusion), channel_id=1, source_target_pairs={{0,8},{8,16},{16,24},{1,9},{9,17},{17,25},{2,10},{10,18},{18,26},{... | collective-permute-start | bytes 122888 | tf_op jit(solution)/shard_map/ppermute | solution.py:510
  7.0 0.0 copy-start.1
  7.0 0.6 copy-done.1
  7.6 0.0 copy-start.4
  7.6 0.8 copy-done.4
  8.5 3.3 %shard_map.94 = (bf16[1024,256]{1,0:T(8,128)(2,1)S(1)}, f32[32,1024]{1,0:T(8,128)S(1)}, f32[8,1024]{1,0:T(8,128)S(1)}) custom-call(s32[4]{0:T(128)S(1)} %copy-done.1, s32[1]{0:T(128)} %bitcast.start_ref, f32[16,1024]{1,0:T(8,128)S(1)} %copy-done.4), custom_call_target="tpu_custom_call" | custom-call | flops 1048576000 | bytes 16777216 | tf_op jit(solution)/shard_map/pallas_call | solution.py:579
  11.8 0.0 copy-start
  11.8 0.0 collective-permute-done.halo_ref
  11.8 0.0 copy-done.2
  11.8 0.0 copy-done.3
  11.9 8.0 %shard_map.95 = (bf16[1024,256]{1,0:T(8,128)(2,1)S(1)}, bf16[1024,256]{1,0:T(8,128)(2,1)S(1)}, f32[1024,256]{1,0:T(8,128)S(1)}, bf16[1024,1024]{1,0:T(8,128)(2,1...) custom-call(s32[4]{0:T(128)S(1)} %copy-done.2, ...), custom_call_target="tpu_custom_call" | custom-call | flops 1048576000 | bytes 16777216 | tf_op jit(solution)/shard_map/pallas_call | solution.py:593
  19.9 0.0 copy-done
  19.9 10.2 %shard_map.96 = (f32[1024,1024]{1,0:T(8,128)S(1)}, bf16[1024,1024]{1,0:T(8,128)(2,1)S(1)}, bf16[1024,1024]{1,0:T(8,128)(2,1)S(1)}, bf16[1024,1024]{1,0:T(8,128)(...) custom-call(s32[4]{0:T(128)S(1)} %copy-done.2, ...), custom_call_target="tpu_custom_call" | custom-call | flops 1048576000 | bytes 16777216 | tf_op jit(solution)/shard_map/pallas_call | solution.py:607
  30.1 1.5 %collective-permute-start.1 = (f32[136,1024]{1,0:T(8,128)S(1)}, f32[136,1024]{1,0:T(8,128)S(1)}, u32[]{:S(2)}, u32[]{:S(2)}) collective-permute-start(f32[136,1024]{1,0:T(8,128)S(1)} %get-tuple-element.59), channel_id=1, source_target_pairs={{0,8},{8,16},{16,24},{24,0},{1,9},{9,17},{17,25},{25,1},{2,10},{10... | collective-permute-start | bytes 1671176 | tf_op jit(solution)/shard_map/ppermute | solution.py:622
  31.7 0.5 collective-permute-start.2
  32.2 2.8 %collective-permute-start.3 = (f32[136,1024]{1,0:T(8,128)S(1)}, f32[136,1024]{1,0:T(8,128)S(1)}, u32[]{:S(2)}, u32[]{:S(2)}) collective-permute-start(f32[136,1024]{1,0:T(8,128)S(1)} %get-tuple-element.61), channel_id=1, source_target_pairs={{0,24},{8,0},{16,8},{24,16},{1,25},{9,1},{17,9},{25,17},{2,26},{10... | collective-permute-start | bytes 1671176 | tf_op jit(solution)/shard_map/ppermute | solution.py:622
  35.1 21.6 %shard_map.97 = (f32[1024,1024]{1,0:T(8,128)S(1)}, f32[1024,256]{1,0:T(8,128)S(1)}, f32[1024,128]{1,0:T(8,128)S(1)}) custom-call(s32[4]{0:T(128)S(1)} %copy-done.2, s32[1]{0:T(128)} %bitcast.start_ref, f32[32,1024]{1,0:T(8,128)S(1)} %get-tuple-element.51.kappa_ref, bf16[1024,1024]{1,0:T(8,128)(2,1)S(1)} %get-tuple-element.52.fx_h.bx_h, ...), custom_call_target="tpu_custom_call" | custom-call | flops 8388608000 | bytes 16777216 | tf_op jit(solution)/shard_map/pallas_call | solution.py:632
  56.7 0.0 collective-permute-done.1.refs_0_
  56.7 0.4 collective-permute-done.2.refs_1_
  57.1 0.5 collective-permute-done.3.refs_2_
  57.6 0.9 %shard_map.98 = (bf16[256,1024]{1,0:T(8,128)(2,1)S(1)}, bf16[256,1024]{1,0:T(8,128)(2,1)S(1)}, f32[8,1024]{1,0:T(8,128)S(1)}, f32[8,1280]{1,0:T(8,128)S(1)}) custom-call(s32[1]{0:T(128)} %bitcast.start_ref, f32[136,1024]{1,0:T(8,128)S(1)} %collective-permute-done.1.refs_0_, f32[136,1024]{1,0:T(8,128)S(1)} %collective-permute-done.2.refs_1_, ...), custom_call_target="tpu_custom_call" | custom-call | flops 209715200 | bytes 16777216 | tf_op jit(solution)/shard_map/pallas_call | solution.py:648
  58.6 1.3 %collective-permute-start.4 = (f32[8,1280]{1,0:T(8,128)S(1)}, f32[8,1280]{1,0:T(8,128)S(1)}, u32[]{:S(2)}, u32[]{:S(2)}) collective-permute-start(f32[8,1280]{1,0:T(8,128)S(1)} %get-tuple-element.67), channel_id=1, source_target_pairs={{8,0},{16,8},{24,16},{9,1},{17,9},{25,17},{10,2},{18,10},{26,18},{... | collective-permute-start | bytes 122888 | tf_op jit(solution)/shard_map/ppermute | solution.py:510
  59.9 2.9 %shard_map.101.shared_ref = f32[1024,256]{1,0:T(8,128)S(1)} custom-call(bf16[1024,1024]{1,0:T(8,128)(2,1)S(1)} %get-tuple-element.44.refs_4_.gh_ref, bf16[1024,1024]{1,0:T(8,128)(2,1)S(1)} %get-tuple-element.45.refs_5_.gl_ref, bf16[1024,1024]{1,0:T(8,128)(2,1)S(1)} %get-tuple-element.49.refs_6_.xh_ref, ...), custom_call_target="tpu_custom_call" | custom-call | flops 1572864000 | bytes 16777216 | tf_op jit(solution)/shard_map/pallas_call | solution.py:672
  62.8 1.6 %collective-permute-done.4.tail_ref.halo_ref = f32[8,1280]{1,0:T(8,128)S(1)} collective-permute-done((f32[8,1280]{1,0:T(8,128)S(1)}, f32[8,1280]{1,0:T(8,128)S(1)}, u32[]{:S(2)}, u32[]{:S(2)}) %collective-permute-start.4) | collective-permute-done | bytes 40992 | tf_op jit(solution)/shard_map/ppermute | solution.py:510
  64.5 1.7 %shard_map.102 = (f32[512,256]{1,0:T(8,128)S(1)}, f32[512,256]{1,0:T(8,128)S(1)}) custom-call(s32[4]{0:T(128)S(1)} %copy-done.2, s32[1]{0:T(128)} %bitcast.start_ref, s32[1]{0:T(128)} %bitcast.1.side_ref, f32[1024,256]{1,0:T(8,128)S(1)} %shard_map.101.shared_ref, f32[8,1280]{1,0:T(8,128)S(1)} %collective-permute-done.4.tail_ref.halo_ref, f32[4,256]{1,0:T(4,128)S(1)} %copy-done.3), custom_call_target="tpu_custom_call" | custom-call | tf_op jit(solution)/shard_map/pallas_call | solution.py:685
  66.1 0.1 collective-permute-start.5
  66.3 1.9 %collective-permute-done.5.came_ref = f32[4,128,256]{2,1,0:T(8,128)S(1)} collective-permute-done((f32[4,128,256]{2,1,0:T(8,128)S(1)}, f32[4,128,256]{2,1,0:T(8,128)S(1)}, u32[]{:S(2)}, u32[]{:S(2)}) %collective-permute-start.5) | collective-permute-done | bytes 524320 | tf_op jit(solution)/shard_map/ppermute | solution.py:527
  68.1 0.1 shard_map.103
  68.2 1.6 %collective-permute-start.6 = (f32[2,128,256]{2,1,0:T(8,128)S(1)}, f32[2,128,256]{2,1,0:T(8,128)S(1)}, u32[]{:S(2)}, u32[]{:S(2)}) collective-permute-start(f32[2,128,256]{2,1,0:T(8,128)S(1)} %get-tuple-element.77), channel_id=1, source_target_pairs={{0,2},{1,3},{2,0},{3,1},{4,6},{5,7},{6,4},{7,5},{8,10},{9,11},{10,... | collective-permute-start | bytes 786440 | tf_op jit(solution)/shard_map/ppermute | solution.py:527
  69.8 7.1 %shard_map.99 = (f32[1024,1024]{1,0:T(8,128)}, f32[16,1024]{1,0:T(8,128)}, f32[8,1024]{1,0:T(8,128)S(1)}, f32[128,128]{1,0:T(8,128)S(1)}) custom-call(s32[4]{0:T(128)S(1)} %copy-done.2, s32[1]{0:T(128)} %bitcast.start_ref, bf16[1024,1024]{1,0:T(8,128)(2,1)S(1)} %get-tuple-element.44.refs_4_.gh_ref, bf16[1024,1024]{1,0:T(8,128)(2,1)S(1)} %get-tuple-element.45.refs_5_.gl_ref, ...), custom_call_target="tpu_custom_call" | custom-call | flops 1572864000 | bytes 16777216 | tf_op jit(solution)/shard_map/pallas_call | solution.py:700
  76.9 0.0 collective-permute-done.6.came_ref
  77.0 2.7 %collective-permute-start.7 = (f32[1,128,256]{2,1,0:T(8,128)S(1)}, f32[1,128,256]{2,1,0:T(8,128)S(1)}, u32[]{:S(2)}, u32[]{:S(2)}) collective-permute-start(f32[1,128,256]{2,1,0:T(8,128)S(1)} %get-tuple-element.79), channel_id=1, source_target_pairs={{0,4},{1,5},{2,6},{3,7},{4,0},{5,1},{6,2},{7,3},{8,12},{9,13},{10,... | collective-permute-start | bytes 393224 | tf_op jit(solution)/shard_map/ppermute | solution.py:527
  79.6 7.0 %shard_map.100 = (f32[1024,1024]{1,0:T(8,128)}, f32[16,1024]{1,0:T(8,128)}, f32[8,1024]{1,0:T(8,128)}, f32[128,128]{1,0:T(8,128)}) custom-call(s32[4]{0:T(128)S(1)} %copy-done.2, s32[1]{0:T(128)} %bitcast.start_ref, bf16[1024,1024]{1,0:T(8,128)(2,1)S(1)} %get-tuple-element.44.refs_4_.gh_ref, ...), custom_call_target="tpu_custom_call", output_to_operand_aliasing={{0}: (17, {}), {1}: (18, {})} | custom-call | flops 1572864000 | bytes 16777216 | tf_op jit(solution)/shard_map/pallas_call | solution.py:700
  86.7 0.0 collective-permute-done.7
  86.7 0.7 shard_map.105
  (2 shorter events, 0.0 us)
Async XLA Ops:
  0.6 11.2 %copy-start.2 = (s32[4]{0:T(128)S(1)}, s32[4]{0:T(128)}, u32[]{:S(2)}) copy-start(s32[4]{0:T(128)} %lens_ref.13) | copy-start | bytes 52
  0.6 11.2 %copy-start.3 = (f32[4,256]{1,0:T(4,128)S(1)}, f32[4,256]{1,0:T(4,128)}, u32[]{:S(2)}) copy-start(f32[4,256]{1,0:T(4,128)} %taps_ref.9) | copy-start | bytes 12292
  2.1 9.7 %collective-permute-start = (bf16[16,1280]{1,0:T(8,128)(2,1)S(1)}, bf16[16,1280]{1,0:T(8,128)(2,1)S(1)}, u32[]{:S(2)}, u32[]{:S(2)}) collective-permute-start(bf16[16,1280]{1,0:T(8,128)(2,1)S(1)} %pad_maximum_fusion), channel_id=1, source_target_pairs={{0,8},{8,16},{16,24},{1,9},{9,17},{17,25},{2,10},{10,18},{18,26},{... | collective-permute-start | bytes 122888 | tf_op jit(solution)/shard_map/ppermute | solution.py:510
  7.0 0.7 copy-start.1
  7.6 0.8 copy-start.4
  11.8 8.1 %copy-start = (f32[4,1024]{1,0:T(4,128)S(1)}, f32[4,1024]{1,0:T(4,128)}, u32[]{:S(2)}) copy-start(f32[4,1024]{1,0:T(4,128)} %taps_ref.8) | copy-start | bytes 49156
  30.1 26.5 %collective-permute-start.1 = (f32[136,1024]{1,0:T(8,128)S(1)}, f32[136,1024]{1,0:T(8,128)S(1)}, u32[]{:S(2)}, u32[]{:S(2)}) collective-permute-start(f32[136,1024]{1,0:T(8,128)S(1)} %get-tuple-element.59), channel_id=1, source_target_pairs={{0,8},{8,16},{16,24},{24,0},{1,9},{9,17},{17,25},{25,1},{2,10},{10... | collective-permute-start | bytes 1671176 | tf_op jit(solution)/shard_map/ppermute | solution.py:622
  31.7 25.4 %collective-permute-start.2 = (f32[136,1024]{1,0:T(8,128)S(1)}, f32[136,1024]{1,0:T(8,128)S(1)}, u32[]{:S(2)}, u32[]{:S(2)}) collective-permute-start(f32[136,1024]{1,0:T(8,128)S(1)} %get-tuple-element.60), channel_id=1, source_target_pairs={{0,16},{8,24},{16,0},{24,8},{1,17},{9,25},{17,1},{25,9},{2,18},{10... | collective-permute-start | bytes 1671176 | tf_op jit(solution)/shard_map/ppermute | solution.py:622
  32.2 25.4 %collective-permute-start.3 = (f32[136,1024]{1,0:T(8,128)S(1)}, f32[136,1024]{1,0:T(8,128)S(1)}, u32[]{:S(2)}, u32[]{:S(2)}) collective-permute-start(f32[136,1024]{1,0:T(8,128)S(1)} %get-tuple-element.61), channel_id=1, source_target_pairs={{0,24},{8,0},{16,8},{24,16},{1,25},{9,1},{17,9},{25,17},{2,26},{10... | collective-permute-start | bytes 1671176 | tf_op jit(solution)/shard_map/ppermute | solution.py:622
  58.6 5.9 %collective-permute-start.4 = (f32[8,1280]{1,0:T(8,128)S(1)}, f32[8,1280]{1,0:T(8,128)S(1)}, u32[]{:S(2)}, u32[]{:S(2)}) collective-permute-start(f32[8,1280]{1,0:T(8,128)S(1)} %get-tuple-element.67), channel_id=1, source_target_pairs={{8,0},{16,8},{24,16},{9,1},{17,9},{25,17},{10,2},{18,10},{26,18},{... | collective-permute-start | bytes 122888 | tf_op jit(solution)/shard_map/ppermute | solution.py:510
  66.1 2.0 %collective-permute-start.5 = (f32[4,128,256]{2,1,0:T(8,128)S(1)}, f32[4,128,256]{2,1,0:T(8,128)S(1)}, u32[]{:S(2)}, u32[]{:S(2)}) collective-permute-start(f32[4,128,256]{2,1,0:T(8,128)S(1)} %bitcast.9), channel_id=1, source_target_pairs={{0,1},{1,0},{2,3},{3,2},{4,5},{5,4},{6,7},{7,6},{8,9},{9,8},{10,11... | collective-permute-start | bytes 1572872 | tf_op jit(solution)/shard_map/ppermute | solution.py:527
  68.2 8.8 %collective-permute-start.6 = (f32[2,128,256]{2,1,0:T(8,128)S(1)}, f32[2,128,256]{2,1,0:T(8,128)S(1)}, u32[]{:S(2)}, u32[]{:S(2)}) collective-permute-start(f32[2,128,256]{2,1,0:T(8,128)S(1)} %get-tuple-element.77), channel_id=1, source_target_pairs={{0,2},{1,3},{2,0},{3,1},{4,6},{5,7},{6,4},{7,5},{8,10},{9,11},{10,... | collective-permute-start | bytes 786440 | tf_op jit(solution)/shard_map/ppermute | solution.py:527
  77.0 9.7 %collective-permute-start.7 = (f32[1,128,256]{2,1,0:T(8,128)S(1)}, f32[1,128,256]{2,1,0:T(8,128)S(1)}, u32[]{:S(2)}, u32[]{:S(2)}) collective-permute-start(f32[1,128,256]{2,1,0:T(8,128)S(1)} %get-tuple-element.79), channel_id=1, source_target_pairs={{0,4},{1,5},{2,6},{3,7},{4,0},{5,1},{6,2},{7,3},{8,12},{9,13},{10,... | collective-permute-start | bytes 393224 | tf_op jit(solution)/shard_map/ppermute | solution.py:527

commit v2 on v1

--- a/solution.py
+++ b/solution.py
@@ -97,23 +97,22 @@
     return total
 
 
-def conv_rows(ext_ref, taps_ref, first, rows, width, position, sign, lens_ref, emit):
+def near_start(position, rows, lens_ref):
     begins = [0, lens_ref[0], lens_ref[0] + lens_ref[1], lens_ref[0] + lens_ref[1] + lens_ref[2]]
     near = [(begin > position - K) & (begin < position + rows + K) for begin in begins]
-    cut = near[0] | near[1] | near[2] | near[3]
-
-    def body(linked):
-        for c in range(0, width, LANES):
-            over = slice(c, c + LANES)
-            emit(over, conv_tile(ext_ref, taps_ref, first, rows, over, linked, sign))
+    return near[0] | near[1] | near[2] | near[3]
+
+
+def two_ways(position, rows, sign, lens_ref, body):
+    cut = near_start(position, rows, lens_ref)
 
     @pl.when(cut)
     def _():
-        body(links(position, rows, sign, lens_ref))
+        body(lambda first, high: links(position + first, high, sign, lens_ref))
 
     @pl.when(jnp.logical_not(cut))
     def _():
-        body(None)
+        body(lambda first, high: None)
 
 
 def silu_and_slope(u):
@@ -131,6 +130,12 @@
 def head_summer(channels):
     same = rows_iota((channels, LANES)) // P_SIZE == cols_iota((channels, LANES))
     return jnp.where(same, 1.0, 0.0).astype(bf16)
+
+
+def edge_kernel(x_ref, bc_ref, edge_ref):
+    channels = x_ref.shape[1]
+    edge_ref[:, :channels] = x_ref[...]
+    edge_ref[:, channels:] = bc_ref[...]
 
 
 def scales_kernel(lens_ref, start_ref, log_ref, scale_ref, kappa_ref, through_ref, padded):
@@ -198,7 +203,7 @@
 def adjoint_kernel(
     lens_ref, start_ref, grad_ref, scale_ref, pre_ref, halo_ref, taps_ref, through_ref,
     hi_ref, lo_ref, slope_ref, rh_ref, rl_ref, gh_ref, gl_ref, send_ref,
-    spread, spread_r, entry, near, ext, *, heads
+    spread, spread_r, ext, *, heads
 ):
     rows, channels = grad_ref.shape
     step = pl.program_id(0)
@@ -217,21 +222,31 @@
 
     ext[8:, :] = pre_ref[...].astype(f32)
     scale = scale_ref[...]
-    entry[...] = dot(scale, spread[...])
-    near[...] = dot(scale, spread_r[...])
-    for first in range(0, rows, 64):
-        at = slice(first, first + 64)
-
-        def emit(over, u, at=at):
-            value, slope_ref[at, over] = silu_and_slope(u)
-            hi_ref[at, over], lo_ref[at, over] = split(value)
-
-        place = start_ref[0] + step * rows + first
-        conv_rows(ext, taps_ref, 8 + first, 64, 2 * N, place, -1, lens_ref, emit)
-    for at, over in tiles(rows, channels):
-        grad = grad_ref[at, over].astype(f32)
-        gh_ref[at, over], gl_ref[at, over] = split(grad * entry[at, over])
-        rh_ref[at, over], rl_ref[at, over] = split(grad * near[at, over])
+    wide = min(2 * LANES, channels)
+
+    def spreads(c):
+        over = slice(c, c + wide)
+        return dot(scale, spread[:, over]), dot(scale, spread_r[:, over])
+
+    def conv(link):
+        for first in range(0, rows, 64):
+            at, linked = slice(first, first + 64), link(first, 64)
+            for c in range(0, 2 * N, LANES):
+                over = slice(c, c + LANES)
+                u = conv_tile(ext, taps_ref, 8 + first, 64, over, linked, -1)
+                value, slope_ref[at, over] = silu_and_slope(u)
+                hi_ref[at, over], lo_ref[at, over] = split(value)
+
+    two_ways(start_ref[0] + step * rows, rows, -1, lens_ref, conv)
+    ready = spreads(0)
+    for c in range(0, channels, wide):
+        entry, near = ready
+        ready = spreads(c + wide) if c + wide < channels else None
+        for at, inside in tiles(rows, wide):
+            over = slice(c + inside.start, c + inside.stop)
+            grad = grad_ref[at, over].astype(f32)
+            gh_ref[at, over], gl_ref[at, over] = split(grad * entry[at, inside])
+            rh_ref[at, over], rl_ref[at, over] = split(grad * near[at, inside])
     send_ref[0:N, :] += dot3_tn((hi_ref[:, N:], lo_ref[:, N:]), (gh_ref[...], gl_ref[...]))
 
 
@@ -240,7 +255,7 @@
     slope_ref, qh_ref, ql_ref, xh_ref, xl_ref, own_ref, *refs, heads, count
 ):
     messages = refs[: count - 1]
-    spread, spread_q, leave, near, ext = refs[count - 1 :]
+    spread, spread_q, ext = refs[count - 1 :]
     rows, channels = pre_ref.shape
     step, steps = pl.program_id(0), pl.num_programs(0)
 
@@ -258,18 +273,26 @@
 
     ext[8:, :] = pre_ref[...].astype(f32)
     scale = scale_ref[...]
-    leave[...] = dot(scale, spread[...])
-    near[...] = dot(scale, spread_q[...])
-    for first in range(0, rows, 64):
-        at = slice(first, first + 64)
-
-        def emit(over, u, at=at):
-            value, slope_ref[at, over] = silu_and_slope(u)
-            xh_ref[at, over], xl_ref[at, over] = split(value * leave[at, over])
-            qh_ref[at, over], ql_ref[at, over] = split(value * near[at, over])
-
-        place = start_ref[0] + step * rows + first
-        conv_rows(ext, taps_ref, 8 + first, 64, channels, place, -1, lens_ref, emit)
+    wide = min(2 * LANES, channels)
+
+    def spreads(c):
+        over = slice(c, c + wide)
+        return dot(scale, spread[:, over]), dot(scale, spread_q[:, over])
+
+    def body(link):
+        ready = spreads(0)
+        linked = [link(first, 64) for first in range(0, rows, 64)]
+        for c in range(0, channels, wide):
+            leave, near = ready
+            ready = spreads(c + wide) if c + wide < channels else None
+            for at, inside in tiles(rows, wide):
+                over = slice(c + inside.start, c + inside.stop)
+                u = conv_tile(ext, taps_ref, 8 + at.start, 64, over, linked[at.start // 64], -1)
+                value, slope_ref[at, over] = silu_and_slope(u)
+                xh_ref[at, over], xl_ref[at, over] = split(value * leave[at, inside])
+                qh_ref[at, over], ql_ref[at, over] = split(value * near[at, inside])
+
+    two_ways(start_ref[0] + step * rows, rows, -1, lens_ref, body)
     own_ref[0:N, :] += dot3_tn((hi_ref[:, :N], lo_ref[:, :N]), (xh_ref[...], xl_ref[...]))
 
     @pl.when(step == steps - 1)
@@ -423,16 +446,18 @@
     ext[0:tokens, :] = shared_ref[...]
     ext[tokens:, :] = halo_ref[:, -2 * N :]
     size = tokens // sharers
-    high = min(size, 64)
+    high = 64
     odd = side_ref[0] % 2 == 1
-    for block in range(sharers):
-        for part in range(0, size, high):
-            first = block * size + part
-
-            def emit(over, value, at=slice(first, first + high)):
-                total[at, over] = value
-
-            conv_rows(ext, taps_ref, first, high, 2 * N, start_ref[0] + first, 1, lens_ref, emit)
+
+    for first in range(0, tokens, high):
+
+        def body(link, at=slice(first, first + high)):
+            linked = link(0, high)
+            for c in range(0, 2 * N, LANES):
+                over = slice(c, c + LANES)
+                total[at, over] = conv_tile(ext, taps_ref, at.start, high, over, linked, 1)
+
+        two_ways(start_ref[0] + first, high, 1, lens_ref, body)
     for pair in range(sharers // 2):
         even, uneven = (total[(2 * pair + i) * size : (2 * pair + i + 1) * size, :] for i in range(2))
         at = slice(pair * size, (pair + 1) * size)
@@ -442,11 +467,9 @@
 
 def final_kernel(
     lens_ref, start_ref, gh_ref, gl_ref, xh_ref, xl_ref, hi_ref, lo_ref, scale_ref,
-    dx_ref, slope_ref, rate_ref, s2_ref, a2_ref, taps_ref, tail_ref, from_ref,
-    *refs, heads, first_block, last
+    dx_ref, slope_ref, rate_ref, s2_ref, a2_ref, taps_ref, tail_ref, end_ref,
+    out_ref, log_ref, carry, spread, spread_q, summer, ext, product, *, heads
 ):
-    out_ref, log_ref, head_ref, carry, spread, spread_q, summer, ext = refs[-13:-5]
-    product, y_tile, dx_tile, near, leave = refs[-5:]
     step = pl.program_id(0)
     rows, channels = gh_ref.shape
 
@@ -456,7 +479,7 @@
         spread_q[...] = expander(heads, channels, 1)
         summer[...] = head_summer(channels)
         ext[rows:, :] = tail_ref[:, :channels]
-        carry[...] = jnp.zeros_like(carry) if last else from_ref[...]
+        carry[...] = jnp.zeros_like(carry)
 
     @pl.when(step > 0)
     def _():
@@ -464,26 +487,33 @@
 
     scale = scale_ref[...]
     wide = min(2 * LANES, channels)
+
+    def products(c):
+        over = slice(c, c + wide)
+        return (
+            push(hi_ref[:, N:], lo_ref[:, N:], s2_ref, over),
+            push(hi_ref[:, :N], lo_ref[:, :N], a2_ref, over),
+            dot(scale, spread_q[:, over]),
+            dot(scale, spread[:, over]),
+        )
+
+    ready = products(0)
     for c in range(0, channels, wide):
-        whole = slice(c, c + wide)
-        y_tile[...] = push(hi_ref[:, N:], lo_ref[:, N:], s2_ref, whole)
-        dx_tile[...] = push(hi_ref[:, :N], lo_ref[:, :N], a2_ref, whole)
-        near[...] = dot(scale, spread_q[:, whole])
-        leave[...] = dot(scale, spread[:, whole])
+        y, entered, near, leave = ready
+        ready = products(c + wide) if c + wide < channels else None
         for at, inside in tiles(rows, wide):
             over = slice(c + inside.start, c + inside.stop)
-            dx = dx_tile[at, inside]
-            rate = whole_of((gh_ref[at, over], gl_ref[at, over])) * y_tile[at, inside]
+            dx = entered[at, inside]
+            rate = whole_of((gh_ref[at, over], gl_ref[at, over])) * y[at, inside]
             rate = rate - whole_of((xh_ref[at, over], xl_ref[at, over])) * dx
             product[at, over], product[rows + at.start : rows + at.stop, over] = split(rate)
             grad = dx_ref[at, over] * near[at, inside] + dx * leave[at, inside]
             ext[at, over] = grad * slope_ref[at, over]
     rates = dot(product[...], summer[...])
     rates = rate_ref[...] + rates[:rows] + rates[rows:]
-    if last:
-        end_row = (rows_iota((rows, LANES)) == rows - 1) & (step == 0)
-        beyond = exact(thirds(from_ref[...]), summer[...])[0:1, :]
-        rates = rates + jnp.where(end_row, beyond, 0.0)
+    end_row = (rows_iota((rows, LANES)) == rows - 1) & (step == 0)
+    beyond = exact(thirds(end_ref[...]), summer[...])[0:1, :]
+    rates = rates + jnp.where(end_row, beyond, 0.0)
     later = rows_iota((rows, rows)) >= cols_iota((rows, rows))
     ones = jnp.ones((rows, LANES), f32)
     marks = jnp.concatenate([jnp.where(later, 1.0, 0.0), ones], axis=1).astype(bf16)
@@ -491,17 +521,16 @@
     log = sums[:, :rows] + widen(carry[...], rows)
     log_ref[...] = log[0:heads, :]
     carry[...] += sums[:, rows:]
-    first = start_ref[0] + (first_block - step) * rows
-    for r in range(0, rows, 64):
-
-        def emit(over, value, at=slice(r, r + 64)):
-            out_ref[at, over] = value
-
-        conv_rows(ext, taps_ref, r, 64, channels, first + r, 1, lens_ref, emit)
-
-    @pl.when(step == pl.num_programs(0) - 1)
-    def _():
-        head_ref[...] = ext[0:8, :]
+    first = start_ref[0] + (pl.num_programs(0) - 1 - step) * rows
+
+    def body(link):
+        for r in range(0, rows, 64):
+            at, linked = slice(r, r + 64), link(r, 64)
+            for c in range(0, channels, LANES):
+                over = slice(c, c + LANES)
+                out_ref[at, over] = conv_tile(ext, taps_ref, r, 64, over, linked, 1)
+
+    two_ways(first, rows, 1, lens_ref, body)
 
 
 def shifted(value, axis, steps):
@@ -518,19 +547,28 @@
         give_ref[pair] = jnp.where(odd, even, uneven)
 
 
-def last_kernel(kept_ref, came_ref, out_ref):
-    out_ref[...] = kept_ref[...] + came_ref[...]
+def pieces_kernel(place_ref, kept_ref, came_ref, *piece_refs):
+    for i, piece_ref in enumerate(piece_refs):
+        block = place_ref[0] ^ i
+        piece_ref[...] = kept_ref[block] + came_ref[block]
+
+
+def total_kernel(*refs):
+    total = refs[0][...]
+    for ref in refs[1:-1]:
+        total = total + ref[...]
+    refs[-1][...] = total
 
 
 def head_scatter(keep, give, mine, params):
     count = lax.axis_size("head")
-    swap = lambda value, bit: lax.ppermute(value, "head", [(i, i ^ bit) for i in range(count)])
+    swap = lambda value, bits: lax.ppermute(value, "head", [(i, i ^ bits) for i in range(count)])
     size, width = 2 * keep.shape[0] // count, keep.shape[1]
     blocks = lambda value: value.reshape(-1, size, width)
     smem = pl.BlockSpec(memory_space=pltpu.SMEM)
     vmem = pl.BlockSpec(memory_space=pltpu.VMEM)
     keep, give, bit = blocks(keep), blocks(give), 1
-    while 2 * bit < count:
+    while keep.shape[0] > 4:
         came = swap(give, bit)
         bit *= 2
         half = jax.ShapeDtypeStruct((keep.shape[0] // 2, size, width), f32)
@@ -541,13 +579,24 @@
             out_specs=(vmem, vmem),
             compiler_params=params,
         )((mine // bit) % 2, keep, came)
+    came = swap(give, bit)
+    bit *= 2
+    left = keep.shape[0]
+    block = jax.ShapeDtypeStruct((size, width), f32)
+    pieces = pl.pallas_call(
+        pieces_kernel,
+        out_shape=(block,) * left,
+        in_specs=[smem, vmem, vmem],
+        out_specs=(vmem,) * left,
+        compiler_params=params,
+    )(mine // bit, keep, came)
     return pl.pallas_call(
-        last_kernel,
-        out_shape=jax.ShapeDtypeStruct((size, width), f32),
-        in_specs=[vmem, vmem],
+        total_kernel,
+        out_shape=block,
+        in_specs=[vmem] * left,
         out_specs=vmem,
         compiler_params=params,
-    )(keep[0], swap(give, bit)[0])
+    )(pieces[0], *[swap(pieces[i], i * bit) for i in range(1, left)])
 
 
 def local(pre_x, pre_bc, conv_x, conv_bc, log_decay, lengths, grad_out):
@@ -561,7 +610,6 @@
     width = 2 * LANES
     start = (lax.axis_index("seq") * tokens).astype(jnp.int32).reshape(1)
     mine = lax.axis_index("head").astype(jnp.int32).reshape(1)
-    halo = shifted(jnp.concatenate([pre_x[-16:], pre_bc[-16:]], axis=1), "seq", 1)
     shape = jax.ShapeDtypeStruct
     smem = pl.BlockSpec(memory_space=pltpu.SMEM)
     vmem = pl.BlockSpec(memory_space=pltpu.VMEM)
@@ -576,6 +624,17 @@
     rows_f32, rows_bf16 = shape((tokens, channels), f32), shape((tokens, channels), bf16)
     bc_f32, bc_bf16 = shape((tokens, 2 * N), f32), shape((tokens, 2 * N), bf16)
 
+    last_rows = lambda cols: pl.BlockSpec((16, cols), lambda i: (tokens // 16 - 1, 0))
+    edge = pl.pallas_call(
+        edge_kernel,
+        grid=(1,),
+        out_shape=shape((16, channels + 2 * N), bf16),
+        in_specs=[last_rows(channels), last_rows(2 * N)],
+        out_specs=whole(16, channels + 2 * N),
+        compiler_params=params,
+    )(pre_x, pre_bc)
+    halo = shifted(edge, "seq", 1)
+
     scale, kappa, through = pl.pallas_call(
         scales_kernel,
         out_shape=(
@@ -589,7 +648,6 @@
     )(lengths, start, log_decay)
 
     spread = pltpu.VMEM((width, channels), bf16)
-    block = pltpu.VMEM((big, channels), f32)
     hi, lo, slope_bc, r_high, r_low, g_high, g_low, send_adjoint = pl.pallas_call(
         functools.partial(adjoint_kernel, heads=heads),
         grid=(steps,),
@@ -599,7 +657,7 @@
             whole(16, channels + 2 * N), whole(K, 2 * N), whole(8, channels),
         ],
         out_specs=(by_rows(big, 2 * N),) * 3 + (by_rows(big, channels),) * 4 + (whole(N + 8, channels),),
-        scratch_shapes=[spread, spread, block, block, pltpu.VMEM((big + 8, 2 * N), f32)],
+        scratch_shapes=[spread, spread, pltpu.VMEM((big + 8, 2 * N), f32)],
         compiler_params=params,
         cost_estimate=cost(1000),
     )(lengths, start, grad_out, scale, pre_bc, halo, conv_bc, through)
@@ -614,7 +672,7 @@
             whole(N + 8, channels),
         ],
         out_specs=(by_rows(big, channels),) * 5 + (whole(N + 8, channels),) * count,
-        scratch_shapes=[spread, spread, block, block, pltpu.VMEM((big + 8, channels), f32)],
+        scratch_shapes=[spread, spread, pltpu.VMEM((big + 8, channels), f32)],
         compiler_params=params,
         cost_estimate=cost(1000),
     )(lengths, start, pre_x, halo, conv_x, scale, hi, lo, through, send_adjoint)
@@ -669,14 +727,15 @@
     )
     after = shifted(head, "seq", -1)
 
+    high = 512
     shared = pl.pallas_call(
         shared_kernel,
-        grid=(steps,),
+        grid=(tokens // high,),
         out_shape=bc_f32,
-        in_specs=[by_rows(big, channels)] * 4
-        + [by_rows(big, 2 * N)] * 2
+        in_specs=[by_rows(high, channels)] * 4
+        + [by_rows(high, 2 * N)] * 2
         + [whole(2 * N, channels)] * 2,
-        out_specs=by_rows(big, 2 * N),
+        out_specs=by_rows(high, 2 * N),
         compiler_params=params,
         cost_estimate=cost(1500),
     )(g_high, g_low, x_high, x_low, dbc, slope_bc, s2, a2)
@@ -692,46 +751,33 @@
     )(lengths, start, mine, shared, after, conv_bc)
     grad_pre_bc = head_scatter(keep, give, mine, params)
 
-    part = steps // 2
-    tail, carry = after, end
-    done = ()
-    for first_block in (steps - 1, steps - 1 - part):
-        back = lambda rows, cols, top=first_block: pl.BlockSpec((rows, cols), lambda i: (top - i, 0))
-        grad_pre_x, grad_log, tail, carry = pl.pallas_call(
-            functools.partial(final_kernel, heads=heads, first_block=first_block, last=not done),
-            grid=(part,),
-            out_shape=(
-                rows_f32, shape((heads, tokens), f32), shape((8, channels), f32),
-                shape((LANES, LANES), f32),
-            ),
-            in_specs=[smem, smem]
-            + [back(big, channels)] * 4
-            + [back(big, 2 * N)] * 2
-            + [back(big, width)]
-            + [back(big, channels)] * 2
-            + [
-                back(big, LANES), whole(2 * N, channels), whole(2 * N, channels),
-                whole(K, channels), whole(*tail.shape), whole(*carry.shape),
-            ]
-            + [pl.BlockSpec(memory_space=pl.ANY)] * len(done),
-            out_specs=(
-                back(big, channels),
-                pl.BlockSpec((heads, big), lambda i, top=first_block: (0, top - i)),
-                whole(8, channels), whole(LANES, LANES),
-            ),
-            scratch_shapes=[
-                spread, spread, pltpu.VMEM((channels, LANES), bf16),
-                pltpu.VMEM((big + 8, channels), f32), pltpu.VMEM((2 * big, channels), bf16),
-            ]
-            + [pltpu.VMEM((big, min(2 * LANES, channels)), f32)] * 4,
-            input_output_aliases={17 + i: i for i in range(len(done))},
-            compiler_params=params,
-            cost_estimate=cost(1500),
-        )(
-            lengths, start, g_high, g_low, x_high, x_low, hi, lo, scale, dx, slope_x, rate, s2, a2,
-            conv_x, tail, carry, *done,
-        )
-        done = (grad_pre_x, grad_log)
+    back = lambda rows, cols: pl.BlockSpec((rows, cols), lambda i: (steps - 1 - i, 0))
+    grad_pre_x, grad_log = pl.pallas_call(
+        functools.partial(final_kernel, heads=heads),
+        grid=(steps,),
+        out_shape=(rows_f32, shape((heads, tokens), f32)),
+        in_specs=[smem, smem]
+        + [back(big, channels)] * 4
+        + [back(big, 2 * N)] * 2
+        + [back(big, width)]
+        + [back(big, channels)] * 2
+        + [
+            back(big, LANES), whole(2 * N, channels), whole(2 * N, channels),
+            whole(K, channels), whole(8, channels + 2 * N), whole(8, channels),
+        ],
+        out_specs=(
+            back(big, channels), pl.BlockSpec((heads, big), lambda i: (0, steps - 1 - i)),
+        ),
+        scratch_shapes=[
+            pltpu.VMEM((LANES, LANES), f32), spread, spread, pltpu.VMEM((channels, LANES), bf16),
+            pltpu.VMEM((big + 8, channels), f32), pltpu.VMEM((2 * big, channels), bf16),
+        ],
+        compiler_params=params,
+        cost_estimate=cost(3000),
+    )(
+        lengths, start, g_high, g_low, x_high, x_low, hi, lo, scale, dx, slope_x, rate, s2, a2,
+        conv_x, after, end,
+    )
     return (grad_pre_x, grad_pre_bc, grad_log)
 
 

time: 87.7 us -> 82.3 us (0.938)
  local copies, waits for them, and re-layouts: 2.97 us -> 0.02 us
  Pallas kernels: 63.7 us -> 60.8 us
    unnamed x10 -> x8, local copies, waits for them, and re-layouts: 1.5 us -> 0.02 us
    pallas_call x1, Pallas kernels: 8.02 us -> 6.54 us  [local(): pl.pallas_call(functools.partial(adjoint_kernel, heads=heads), grid=(step...]
    slice x2 -> x0, local copies, waits for them, and re-layouts: 1.47 us -> none  [the longest x1 0.77 us: local(): pre_x[-16:]]
    pallas_call x6 -> x5, Pallas kernels: 17.9 us -> 17.2 us  [the longest x1 13 us: local(): pl.pallas_call(functools.partial(final_kernel, heads=heads), grid=(steps,...]
    ppermute x3 -> x4, starting transfers between devices: 4.37 us -> 4.52 us  [head_scatter(): lax.ppermute(value, 'head', [(i, i ^ bits) for i in range(count)])]
    ppermute x3 -> x4, waiting for transfers between devices: 1.87 us -> 1.89 us  [head_scatter(): lax.ppermute(value, 'head', [(i, i ^ bits) for i in range(count)])]
  transfers between devices with their start and end apart: 8 -> 9, of which waited for: 4 -> 4; matrix products, arithmetic and copies ran while one was open for 0% -> 0% of each run, Pallas kernels for 48% -> 50%
where the time goes in v2:
time: 82.3 us; the launch traced here: 81.6 us
  Pallas kernels  60.8 us (74%)
  starting transfers between devices  15.5 us (19%)
  waiting for transfers between devices  4.54 us (6%)
    pallas_call x1, Pallas kernels, local(): pl.pallas_call(local_kernel, grid=(chunks,), out_shape=(rows_f32, bc_f32,...  21.6 us
    pallas_call x1, Pallas kernels, local(): pl.pallas_call(functools.partial(final_kernel, heads=heads), grid=(steps,...  13 us
    pallas_call x1, Pallas kernels, local(): pl.pallas_call(functools.partial(state_kernel, heads=heads, count=count),...  9.61 us
    pallas_call x1, Pallas kernels, local(): pl.pallas_call(functools.partial(adjoint_kernel, heads=heads), grid=(step...  6.54 us
    ppermute x2, starting transfers between devices, shifted(): lax.ppermute(value, axis, [(source, source + steps) for source in range(i...  6.44 us
    ppermute x4, starting transfers between devices, head_scatter(): lax.ppermute(value, 'head', [(i, i ^ bits) for i in range(count)])  4.52 us
    ppermute x3, starting transfers between devices, local(): lax.ppermute(message, 'seq', [(i, (i + lag) % count) for i in range(count)])  4.52 us
    pallas_call x1, Pallas kernels, local(): pl.pallas_call(scales_kernel, out_shape=(shape((tokens, width), bf16), sh...  3.35 us
  transfers between devices with their start and end apart: 9, of which 4 were waited for; matrix products, arithmetic and copies ran while one was open for 0% of the time, Pallas kernels for 50%

profile of v2, /device:TPU:0, one launch (start us, length us, event | category | flops | bytes accessed | tf_op | source)
XLA Modules:
  0.0 81.6 jit_solution(10174198896805144134)
XLA Ops:
  0.6 0.0 copy-start.3
  0.6 0.0 copy-start.1
  0.7 0.8 shard_map.95
  1.4 0.0 copy-start.2
  1.4 5.0 %collective-permute-start = (bf16[16,1280]{1,0:T(8,128)(2,1)S(1)}, bf16[16,1280]{1,0:T(8,128)(2,1)S(1)}, u32[]{:S(2)}, u32[]{:S(2)}) collective-permute-start(bf16[16,1280]{1,0:T(8,128)(2,1)S(1)} %shard_map.95), channel_id=1, source_target_pairs={{0,8},{8,16},{16,24},{1,9},{9,17},{17,25},{2,10},{10,18},{18,26},{... | collective-permute-start | bytes 122888 | tf_op jit(solution)/shard_map/ppermute | solution.py:539
  6.4 0.0 copy-done.3
  6.4 0.0 copy-done.1
  6.4 3.3 %shard_map.94 = (bf16[1024,256]{1,0:T(8,128)(2,1)S(1)}, f32[32,1024]{1,0:T(8,128)S(1)}, f32[8,1024]{1,0:T(8,128)S(1)}) custom-call(s32[4]{0:T(128)S(1)} %copy-done.1, s32[1]{0:T(128)} %bitcast.start_ref, f32[16,1024]{1,0:T(8,128)S(1)} %copy-done.3), custom_call_target="tpu_custom_call" | custom-call | flops 1048576000 | bytes 16777216 | tf_op jit(solution)/shard_map/pallas_call | solution.py:638
  9.8 0.0 copy-start
  9.8 0.0 collective-permute-done.halo_ref
  9.8 0.0 copy-done.2
  9.8 6.5 %shard_map.96 = (bf16[1024,256]{1,0:T(8,128)(2,1)S(1)}, bf16[1024,256]{1,0:T(8,128)(2,1)S(1)}, f32[1024,256]{1,0:T(8,128)S(1)}, bf16[1024,1024]{1,0:T(8,128)(2,1...) custom-call(s32[4]{0:T(128)S(1)} %copy-done.1, ...), custom_call_target="tpu_custom_call" | custom-call | flops 1048576000 | bytes 16777216 | tf_op jit(solution)/shard_map/pallas_call | solution.py:651
  16.4 0.0 copy-done
  16.4 9.6 %shard_map.97 = (f32[1024,1024]{1,0:T(8,128)S(1)}, bf16[1024,1024]{1,0:T(8,128)(2,1)S(1)}, bf16[1024,1024]{1,0:T(8,128)(2,1)S(1)}, bf16[1024,1024]{1,0:T(8,128)(...) custom-call(s32[4]{0:T(128)S(1)} %copy-done.1, ...), custom_call_target="tpu_custom_call" | custom-call | flops 1048576000 | bytes 16777216 | tf_op jit(solution)/shard_map/pallas_call | solution.py:665
  26.0 1.5 %collective-permute-start.1 = (f32[136,1024]{1,0:T(8,128)S(1)}, f32[136,1024]{1,0:T(8,128)S(1)}, u32[]{:S(2)}, u32[]{:S(2)}) collective-permute-start(f32[136,1024]{1,0:T(8,128)S(1)} %get-tuple-element.55), channel_id=1, source_target_pairs={{0,8},{8,16},{16,24},{24,0},{1,9},{9,17},{17,25},{25,1},{2,10},{10... | collective-permute-start | bytes 1671176 | tf_op jit(solution)/shard_map/ppermute | solution.py:680
  27.5 1.5 %collective-permute-start.2 = (f32[136,1024]{1,0:T(8,128)S(1)}, f32[136,1024]{1,0:T(8,128)S(1)}, u32[]{:S(2)}, u32[]{:S(2)}) collective-permute-start(f32[136,1024]{1,0:T(8,128)S(1)} %get-tuple-element.56), channel_id=1, source_target_pairs={{0,16},{8,24},{16,0},{24,8},{1,17},{9,25},{17,1},{25,9},{2,18},{10... | collective-permute-start | bytes 1671176 | tf_op jit(solution)/shard_map/ppermute | solution.py:680
  29.1 1.5 %collective-permute-start.3 = (f32[136,1024]{1,0:T(8,128)S(1)}, f32[136,1024]{1,0:T(8,128)S(1)}, u32[]{:S(2)}, u32[]{:S(2)}) collective-permute-start(f32[136,1024]{1,0:T(8,128)S(1)} %get-tuple-element.57), channel_id=1, source_target_pairs={{0,24},{8,0},{16,8},{24,16},{1,25},{9,1},{17,9},{25,17},{2,26},{10... | collective-permute-start | bytes 1671176 | tf_op jit(solution)/shard_map/ppermute | solution.py:680
  30.5 21.6 %shard_map.98 = (f32[1024,1024]{1,0:T(8,128)S(1)}, f32[1024,256]{1,0:T(8,128)S(1)}, f32[1024,128]{1,0:T(8,128)S(1)}) custom-call(s32[4]{0:T(128)S(1)} %copy-done.1, s32[1]{0:T(128)} %bitcast.start_ref, f32[32,1024]{1,0:T(8,128)S(1)} %get-tuple-element.47.kappa_ref, bf16[1024,1024]{1,0:T(8,128)(2,1)S(1)} %get-tuple-element.48.fx_h.bx_h, ...), custom_call_target="tpu_custom_call" | custom-call | flops 8388608000 | bytes 16777216 | tf_op jit(solution)/shard_map/pallas_call | solution.py:690
  52.2 0.0 collective-permute-done.1.refs_0_
  52.2 0.8 collective-permute-done.2.refs_1_
  53.0 0.1 collective-permute-done.3.refs_2_
  53.1 0.9 %shard_map.99 = (bf16[256,1024]{1,0:T(8,128)(2,1)S(1)}, bf16[256,1024]{1,0:T(8,128)(2,1)S(1)}, f32[8,1024]{1,0:T(8,128)S(1)}, f32[8,1280]{1,0:T(8,128)S(1)}) custom-call(s32[1]{0:T(128)} %bitcast.start_ref, f32[136,1024]{1,0:T(8,128)S(1)} %collective-permute-done.1.refs_0_, f32[136,1024]{1,0:T(8,128)S(1)} %collective-permute-done.2.refs_1_, ...), custom_call_target="tpu_custom_call" | custom-call | flops 209715200 | bytes 16777216 | tf_op jit(solution)/shard_map/pallas_call | solution.py:706
  54.0 1.5 %collective-permute-start.4 = (f32[8,1280]{1,0:T(8,128)S(1)}, f32[8,1280]{1,0:T(8,128)S(1)}, u32[]{:S(2)}, u32[]{:S(2)}) collective-permute-start(f32[8,1280]{1,0:T(8,128)S(1)} %get-tuple-element.63), channel_id=1, source_target_pairs={{8,0},{16,8},{24,16},{9,1},{17,9},{25,17},{10,2},{18,10},{26,18},{... | collective-permute-start | bytes 122888 | tf_op jit(solution)/shard_map/ppermute | solution.py:539
  55.5 2.7 %shard_map.101.shared_ref = f32[1024,256]{1,0:T(8,128)S(1)} custom-call(bf16[1024,1024]{1,0:T(8,128)(2,1)S(1)} %get-tuple-element.40.refs_4_.gh_ref, bf16[1024,1024]{1,0:T(8,128)(2,1)S(1)} %get-tuple-element.41.refs_5_.gl_ref, bf16[1024,1024]{1,0:T(8,128)(2,1)S(1)} %get-tuple-element.45.refs_6_.xh_ref, ...), custom_call_target="tpu_custom_call" | custom-call | flops 1572864000 | bytes 16777216 | tf_op jit(solution)/shard_map/pallas_call | solution.py:731
  58.2 1.7 %collective-permute-done.4.tail_ref.halo_ref = f32[8,1280]{1,0:T(8,128)S(1)} collective-permute-done((f32[8,1280]{1,0:T(8,128)S(1)}, f32[8,1280]{1,0:T(8,128)S(1)}, u32[]{:S(2)}, u32[]{:S(2)}) %collective-permute-start.4) | collective-permute-done | bytes 40992 | tf_op jit(solution)/shard_map/ppermute | solution.py:539
  59.9 1.5 %shard_map.102 = (f32[512,256]{1,0:T(8,128)S(1)}, f32[512,256]{1,0:T(8,128)S(1)}) custom-call(s32[4]{0:T(128)S(1)} %copy-done.1, s32[1]{0:T(128)} %bitcast.start_ref, s32[1]{0:T(128)} %bitcast.1.side_ref, f32[1024,256]{1,0:T(8,128)S(1)} %shard_map.101.shared_ref, f32[8,1280]{1,0:T(8,128)S(1)} %collective-permute-done.4.tail_ref.halo_ref, f32[4,256]{1,0:T(4,128)S(1)} %copy-done.2), custom_call_target="tpu_custom_call" | custom-call | tf_op jit(solution)/shard_map/pallas_call | solution.py:744
  61.4 0.1 collective-permute-start.5
  61.5 1.9 %collective-permute-done.5.came_ref = f32[4,128,256]{2,1,0:T(8,128)S(1)} collective-permute-done((f32[4,128,256]{2,1,0:T(8,128)S(1)}, f32[4,128,256]{2,1,0:T(8,128)S(1)}, u32[]{:S(2)}, u32[]{:S(2)}) %collective-permute-start.5) | collective-permute-done | bytes 524320 | tf_op jit(solution)/shard_map/ppermute | solution.py:565
  63.4 0.1 shard_map.103
  63.5 1.6 %collective-permute-start.6 = (f32[128,256]{1,0:T(8,128)S(1)}, f32[128,256]{1,0:T(8,128)S(1)}, u32[]{:S(2)}, u32[]{:S(2)}) collective-permute-start(f32[128,256]{1,0:T(8,128)S(1)} %get-tuple-element.69), channel_id=1, source_target_pairs={{0,2},{1,3},{2,0},{3,1},{4,6},{5,7},{6,4},{7,5},{8,10},{9,11},{10,... | collective-permute-start | bytes 393224 | tf_op jit(solution)/shard_map/ppermute | solution.py:565
  65.1 2.6 %collective-permute-start.7 = (f32[128,256]{1,0:T(8,128)S(1)}, f32[128,256]{1,0:T(8,128)S(1)}, u32[]{:S(2)}, u32[]{:S(2)}) collective-permute-start(f32[128,256]{1,0:T(8,128)S(1)} %get-tuple-element.70), channel_id=1, source_target_pairs={{0,4},{1,5},{2,6},{3,7},{4,0},{5,1},{6,2},{7,3},{8,12},{9,13},{10,... | collective-permute-start | bytes 393224 | tf_op jit(solution)/shard_map/ppermute | solution.py:565
  67.7 0.2 collective-permute-start.8
  67.9 13.0 %shard_map.100 = (f32[1024,1024]{1,0:T(8,128)}, f32[16,1024]{1,0:T(8,128)}) custom-call(s32[4]{0:T(128)S(1)} %copy-done.1, s32[1]{0:T(128)} %bitcast.start_ref, bf16[1024,1024]{1,0:T(8,128)(2,1)S(1)} %get-tuple-element.40.refs_4_.gh_ref, bf16[1024,1024]{1,0:T(8,128)(2,1)S(1)} %get-tuple-element.41.refs_5_.gl_ref, ...), custom_call_target="tpu_custom_call" | custom-call | flops 3145728000 | bytes 16777216 | tf_op jit(solution)/shard_map/pallas_call | solution.py:755
  80.9 0.0 collective-permute-done.6.refs_1_
  80.9 0.0 collective-permute-done.7.refs_2_
  80.9 0.0 collective-permute-done.8.refs_3_
  80.9 0.7 shard_map.104
Async XLA Ops:
  0.6 5.8 %copy-start.3 = (f32[16,1024]{1,0:T(8,128)S(1)}, f32[16,1024]{1,0:T(8,128)}, u32[]{:S(2)}) copy-start(f32[16,1024]{1,0:T(8,128)} %log_ref.1) | copy-start | bytes 196612
  0.6 5.8 %copy-start.1 = (s32[4]{0:T(128)S(1)}, s32[4]{0:T(128)}, u32[]{:S(2)}) copy-start(s32[4]{0:T(128)} %lens_ref.11) | copy-start | bytes 52
  1.4 8.4 %copy-start.2 = (f32[4,256]{1,0:T(4,128)S(1)}, f32[4,256]{1,0:T(4,128)}, u32[]{:S(2)}) copy-start(f32[4,256]{1,0:T(4,128)} %taps_ref.7) | copy-start | bytes 12292
  1.4 8.4 %collective-permute-start = (bf16[16,1280]{1,0:T(8,128)(2,1)S(1)}, bf16[16,1280]{1,0:T(8,128)(2,1)S(1)}, u32[]{:S(2)}, u32[]{:S(2)}) collective-permute-start(bf16[16,1280]{1,0:T(8,128)(2,1)S(1)} %shard_map.95), channel_id=1, source_target_pairs={{0,8},{8,16},{16,24},{1,9},{9,17},{17,25},{2,10},{10,18},{18,26},{... | collective-permute-start | bytes 122888 | tf_op jit(solution)/shard_map/ppermute | solution.py:539
  9.8 6.6 %copy-start = (f32[4,1024]{1,0:T(4,128)S(1)}, f32[4,1024]{1,0:T(4,128)}, u32[]{:S(2)}) copy-start(f32[4,1024]{1,0:T(4,128)} %taps_ref.6) | copy-start | bytes 49156
  26.0 26.2 %collective-permute-start.1 = (f32[136,1024]{1,0:T(8,128)S(1)}, f32[136,1024]{1,0:T(8,128)S(1)}, u32[]{:S(2)}, u32[]{:S(2)}) collective-permute-start(f32[136,1024]{1,0:T(8,128)S(1)} %get-tuple-element.55), channel_id=1, source_target_pairs={{0,8},{8,16},{16,24},{24,0},{1,9},{9,17},{17,25},{25,1},{2,10},{10... | collective-permute-start | bytes 1671176 | tf_op jit(solution)/shard_map/ppermute | solution.py:680
  27.5 25.4 %collective-permute-start.2 = (f32[136,1024]{1,0:T(8,128)S(1)}, f32[136,1024]{1,0:T(8,128)S(1)}, u32[]{:S(2)}, u32[]{:S(2)}) collective-permute-start(f32[136,1024]{1,0:T(8,128)S(1)} %get-tuple-element.56), channel_id=1, source_target_pairs={{0,16},{8,24},{16,0},{24,8},{1,17},{9,25},{17,1},{25,9},{2,18},{10... | collective-permute-start | bytes 1671176 | tf_op jit(solution)/shard_map/ppermute | solution.py:680
  29.1 24.0 %collective-permute-start.3 = (f32[136,1024]{1,0:T(8,128)S(1)}, f32[136,1024]{1,0:T(8,128)S(1)}, u32[]{:S(2)}, u32[]{:S(2)}) collective-permute-start(f32[136,1024]{1,0:T(8,128)S(1)} %get-tuple-element.57), channel_id=1, source_target_pairs={{0,24},{8,0},{16,8},{24,16},{1,25},{9,1},{17,9},{25,17},{2,26},{10... | collective-permute-start | bytes 1671176 | tf_op jit(solution)/shard_map/ppermute | solution.py:680
  54.0 5.9 %collective-permute-start.4 = (f32[8,1280]{1,0:T(8,128)S(1)}, f32[8,1280]{1,0:T(8,128)S(1)}, u32[]{:S(2)}, u32[]{:S(2)}) collective-permute-start(f32[8,1280]{1,0:T(8,128)S(1)} %get-tuple-element.63), channel_id=1, source_target_pairs={{8,0},{16,8},{24,16},{9,1},{17,9},{25,17},{10,2},{18,10},{26,18},{... | collective-permute-start | bytes 122888 | tf_op jit(solution)/shard_map/ppermute | solution.py:539
  61.4 2.0 %collective-permute-start.5 = (f32[4,128,256]{2,1,0:T(8,128)S(1)}, f32[4,128,256]{2,1,0:T(8,128)S(1)}, u32[]{:S(2)}, u32[]{:S(2)}) collective-permute-start(f32[4,128,256]{2,1,0:T(8,128)S(1)} %bitcast.5), channel_id=1, source_target_pairs={{0,1},{1,0},{2,3},{3,2},{4,5},{5,4},{6,7},{7,6},{8,9},{9,8},{10,11... | collective-permute-start | bytes 1572872 | tf_op jit(solution)/shard_map/ppermute | solution.py:565
  63.5 17.4 %collective-permute-start.6 = (f32[128,256]{1,0:T(8,128)S(1)}, f32[128,256]{1,0:T(8,128)S(1)}, u32[]{:S(2)}, u32[]{:S(2)}) collective-permute-start(f32[128,256]{1,0:T(8,128)S(1)} %get-tuple-element.69), channel_id=1, source_target_pairs={{0,2},{1,3},{2,0},{3,1},{4,6},{5,7},{6,4},{7,5},{8,10},{9,11},{10,... | collective-permute-start | bytes 393224 | tf_op jit(solution)/shard_map/ppermute | solution.py:565
  65.1 15.8 %collective-permute-start.7 = (f32[128,256]{1,0:T(8,128)S(1)}, f32[128,256]{1,0:T(8,128)S(1)}, u32[]{:S(2)}, u32[]{:S(2)}) collective-permute-start(f32[128,256]{1,0:T(8,128)S(1)} %get-tuple-element.70), channel_id=1, source_target_pairs={{0,4},{1,5},{2,6},{3,7},{4,0},{5,1},{6,2},{7,3},{8,12},{9,13},{10,... | collective-permute-start | bytes 393224 | tf_op jit(solution)/shard_map/ppermute | solution.py:565
  67.7 13.2 %collective-permute-start.8 = (f32[128,256]{1,0:T(8,128)S(1)}, f32[128,256]{1,0:T(8,128)S(1)}, u32[]{:S(2)}, u32[]{:S(2)}) collective-permute-start(f32[128,256]{1,0:T(8,128)S(1)} %get-tuple-element.71), channel_id=1, source_target_pairs={{0,6},{1,7},{2,4},{3,5},{4,2},{5,3},{6,0},{7,1},{8,14},{9,15},{10,... | collective-permute-start | bytes 393224 | tf_op jit(solution)/shard_map/ppermute | solution.py:565

commit v3 on v2

--- a/solution.py
+++ b/solution.py
@@ -299,13 +299,17 @@
     def _():
         for lag in range(1, count):
             ahead = start_ref[0] + lag * rows * steps < count * rows * steps
-            messages[lag - 1][...] = jnp.where(ahead, own_ref[...], other_ref[...])
+            for part in range(channels // LANES):
+                over, at = slice(part * LANES, (part + 1) * LANES), N * part
+                held = jnp.where(ahead, own_ref[:, over], other_ref[:, over])
+                messages[lag - 1][at : at + N, :] = held[:N]
+                messages[lag - 1][N * channels // LANES + part : N * channels // LANES + part + 1, :] = held[N : N + 1]
 
 
 def local_kernel(
     lens_ref, start_ref, kappa_ref,
     fx_h, fx_l, fg_h, fg_l, f_hi, f_lo, bx_h, bx_l, bg_h, bg_l, b_hi, b_lo,
-    dx_ref, dbc_ref, rate_ref, state, adjoint, summer, product
+    scale_ref, dx_ref, dbc_ref, rate_ref, state, adjoint, summer, product, spread, *, heads
 ):
     step = pl.program_id(0)
     chunks = pl.num_programs(0)
@@ -315,6 +319,7 @@
     @pl.when(step == 0)
     def _():
         summer[...] = head_summer(channels)
+        spread[...] = expander(heads, channels, 1)
         state[...] = jnp.zeros_like(state)
         adjoint[...] = jnp.zeros_like(adjoint)
         dbc_ref[...] = jnp.zeros_like(dbc_ref)
@@ -372,7 +377,8 @@
         before = jnp.maximum(there - 1, 0)
         dx, _, a_parts = walk(adjoint, b_left, b_turn, (bg_h, bg_l), b_keep, before, over)
         outer = outer + dot3((bx_h[:, over], bx_l[:, over]), a_parts, NT)
-        dx_ref[:, over] = dx + own * whole_of((bg_h[:, over], bg_l[:, over]))
+        near = dot(scale_ref[...], spread[:, over])
+        dx_ref[:, over] = (dx + own * whole_of((bg_h[:, over], bg_l[:, over]))) * near
         product[2 * CHUNK : 3 * CHUNK, over], product[3 * CHUNK :, over] = split(
             whole_of((bx_h[:, over], bx_l[:, over])) * dx
         )
@@ -387,10 +393,15 @@
 
 
 def joined(messages):
-    total = jnp.zeros((N, messages[0].shape[1]), f32)
-    for message in reversed(messages):
-        total = message[0:N, :] + message[N : N + 1, :] * total
-    return total
+    parts = (messages[0].shape[0] - 8) // N
+    tiles_of = []
+    for part in range(parts):
+        total = jnp.zeros((N, LANES), f32)
+        for message in reversed(messages):
+            through = message[N * parts + part : N * parts + part + 1, :]
+            total = message[part * N : (part + 1) * N, :] + through * total
+        tiles_of.append(total)
+    return jnp.concatenate(tiles_of, axis=1)
 
 
 def pull(high, low, both):
@@ -427,8 +438,8 @@
     for_b = pull(xh_ref[...], xl_ref[...], a2_ref)
     shared = (dbc_ref[...] + jnp.concatenate([for_b, for_c], axis=1)) * slope_bc_ref[...]
     scale = scale_ref[...]
-    dx = dx_ref[...] * dot(scale, expander(heads, channels, 1))
-    dx = dx + push(hi_ref[:, :N], lo_ref[:, :N], a2_ref) * dot(scale, expander(heads, channels, 3))
+    dx = push(hi_ref[:, :N], lo_ref[:, :N], a2_ref) * dot(scale, expander(heads, channels, 3))
+    dx = dx_ref[...] + dx
     head_ref[:, :channels] = (dx * slope_ref[...])[0:8, :]
     head_ref[:, channels:] = shared[0:8, :]
 
@@ -468,7 +479,7 @@
 def final_kernel(
     lens_ref, start_ref, gh_ref, gl_ref, xh_ref, xl_ref, hi_ref, lo_ref, scale_ref,
     dx_ref, slope_ref, rate_ref, s2_ref, a2_ref, taps_ref, tail_ref, end_ref,
-    out_ref, log_ref, carry, spread, spread_q, summer, ext, product, *, heads
+    out_ref, log_ref, carry, spread, summer, ext, product, *, heads
 ):
     step = pl.program_id(0)
     rows, channels = gh_ref.shape
@@ -476,7 +487,6 @@
     @pl.when(step == 0)
     def _():
         spread[...] = expander(heads, channels, 3)
-        spread_q[...] = expander(heads, channels, 1)
         summer[...] = head_summer(channels)
         ext[rows:, :] = tail_ref[:, :channels]
         carry[...] = jnp.zeros_like(carry)
@@ -493,13 +503,12 @@
         return (
             push(hi_ref[:, N:], lo_ref[:, N:], s2_ref, over),
             push(hi_ref[:, :N], lo_ref[:, :N], a2_ref, over),
-            dot(scale, spread_q[:, over]),
             dot(scale, spread[:, over]),
         )
 
     ready = products(0)
     for c in range(0, channels, wide):
-        y, entered, near, leave = ready
+        y, entered, leave = ready
         ready = products(c + wide) if c + wide < channels else None
         for at, inside in tiles(rows, wide):
             over = slice(c + inside.start, c + inside.stop)
@@ -507,7 +516,7 @@
             rate = whole_of((gh_ref[at, over], gl_ref[at, over])) * y[at, inside]
             rate = rate - whole_of((xh_ref[at, over], xl_ref[at, over])) * dx
             product[at, over], product[rows + at.start : rows + at.stop, over] = split(rate)
-            grad = dx_ref[at, over] * near[at, inside] + dx * leave[at, inside]
+            grad = dx_ref[at, over] + dx * leave[at, inside]
             ext[at, over] = grad * slope_ref[at, over]
     rates = dot(product[...], summer[...])
     rates = rate_ref[...] + rates[:rows] + rates[rows:]
@@ -662,16 +671,21 @@
         cost_estimate=cost(1000),
     )(lengths, start, grad_out, scale, pre_bc, halo, conv_bc, through)
 
+    packed = (N * channels // LANES + 8, LANES)
     slope_x, q_high, q_low, x_high, x_low, own_state, *messages = pl.pallas_call(
         functools.partial(state_kernel, heads=heads, count=count),
         grid=(steps,),
-        out_shape=(rows_f32,) + (rows_bf16,) * 4 + (shape((N + 8, channels), f32),) * count,
+        out_shape=(rows_f32,) + (rows_bf16,) * 4
+        + (shape((N + 8, channels), f32),)
+        + (shape(packed, f32),) * (count - 1),
         in_specs=[
             smem, smem, by_rows(big, channels), whole(16, channels + 2 * N), whole(K, channels),
             by_rows(big, width), by_rows(big, 2 * N), by_rows(big, 2 * N), whole(8, channels),
             whole(N + 8, channels),
         ],
-        out_specs=(by_rows(big, channels),) * 5 + (whole(N + 8, channels),) * count,
+        out_specs=(by_rows(big, channels),) * 5
+        + (whole(N + 8, channels),)
+        + (whole(*packed),) * (count - 1),
         scratch_shapes=[spread, spread, pltpu.VMEM((big + 8, channels), f32)],
         compiler_params=params,
         cost_estimate=cost(1000),
@@ -688,21 +702,20 @@
         for size in (channels, channels, channels, channels, 2 * N, 2 * N)
     ]
     dx, dbc, rate = pl.pallas_call(
-        local_kernel,
+        functools.partial(local_kernel, heads=heads),
         grid=(chunks,),
         out_shape=(rows_f32, bc_f32, shape((tokens, LANES), f32)),
-        in_specs=[smem, smem, whole(2 * chunks, channels)] + both_ways,
+        in_specs=[smem, smem, whole(2 * chunks, channels)] + both_ways + [from_end(CHUNK, width)],
         out_specs=(from_end(CHUNK, channels), whole(tokens, 2 * N), whole(tokens, LANES)),
         scratch_shapes=[
             pltpu.VMEM((N, channels), f32), pltpu.VMEM((N, channels), f32),
             pltpu.VMEM((channels, LANES), bf16),
         ]
-        + [pltpu.VMEM((4 * CHUNK, channels), bf16)],
+        + [pltpu.VMEM((4 * CHUNK, channels), bf16), spread],
         compiler_params=params,
         cost_estimate=cost(8000),
-    )(lengths, start, kappa, *([q_high, q_low, r_high, r_low, hi, lo] * 2))
-
-    message = whole(N + 8, channels)
+    )(lengths, start, kappa, *([q_high, q_low, r_high, r_low, hi, lo] * 2), scale)
+
     s2, a2, end, head = pl.pallas_call(
         functools.partial(entering_kernel, count=count, heads=heads, tokens=tokens),
         grid=(1,),
@@ -711,7 +724,8 @@
             shape((8, channels + 2 * N), f32),
         ),
         in_specs=[smem]
-        + [message] * count
+        + [whole(*packed)] * (count - 1)
+        + [whole(N + 8, channels)]
         + [whole(16, channels)] * 4
         + [whole(16, 2 * N)] * 2
         + [whole(16, width), whole(16, channels), whole(16, 2 * N), whole(16, channels), whole(16, 2 * N)],
@@ -769,7 +783,7 @@
             back(big, channels), pl.BlockSpec((heads, big), lambda i: (0, steps - 1 - i)),
         ),
         scratch_shapes=[
-            pltpu.VMEM((LANES, LANES), f32), spread, spread, pltpu.VMEM((channels, LANES), bf16),
+            pltpu.VMEM((LANES, LANES), f32), spread, pltpu.VMEM((channels, LANES), bf16),
             pltpu.VMEM((big + 8, channels), f32), pltpu.VMEM((2 * big, channels), bf16),
         ],
         compiler_params=params,

time: 82.3 us -> 83 us (level)
  Pallas kernels: 60.8 us -> 61.9 us
  starting transfers between devices: 15.5 us -> 16.4 us
  waiting for transfers between devices: 4.54 us -> 3.71 us
    pallas_call x1, Pallas kernels: 21.6 us -> 23.7 us  [local(): pl.pallas_call(functools.partial(local_kernel, heads=heads), grid=(chunks...]
    ppermute x3, starting transfers between devices: 4.52 us -> 5.44 us  [local(): lax.ppermute(message, 'seq', [(i, (i + lag) % count) for i in range(count)])]
    ppermute x3, waiting for transfers between devices: 0.9 us -> 0.01 us  [local(): lax.ppermute(message, 'seq', [(i, (i + lag) % count) for i in range(count)])]
    pallas_call x1, Pallas kernels: 13 us -> 12.1 us  [local(): pl.pallas_call(functools.partial(final_kernel, heads=heads), grid=(steps,...]
  transfers between devices with their start and end apart: 9 -> 9, of which waited for: 4 -> 2; matrix products, arithmetic and copies ran while one was open for 0% -> 0% of each run, Pallas kernels for 50% -> 50%
where the time goes in v3:
time: 83 us; the launch traced here: 82.9 us
  Pallas kernels  61.9 us (75%)
  starting transfers between devices  16.4 us (20%)
  waiting for transfers between devices  3.71 us (4%)
    pallas_call x1, Pallas kernels, local(): pl.pallas_call(functools.partial(local_kernel, heads=heads), grid=(chunks...  23.7 us
    pallas_call x1, Pallas kernels, local(): pl.pallas_call(functools.partial(final_kernel, heads=heads), grid=(steps,...  12.1 us
    pallas_call x1, Pallas kernels, local(): pl.pallas_call(functools.partial(state_kernel, heads=heads, count=count),...  9.61 us
    pallas_call x1, Pallas kernels, local(): pl.pallas_call(functools.partial(adjoint_kernel, heads=heads), grid=(step...  6.57 us
    ppermute x2, starting transfers between devices, shifted(): lax.ppermute(value, axis, [(source, source + steps) for source in range(i...  6.44 us
    ppermute x3, starting transfers between devices, local(): lax.ppermute(message, 'seq', [(i, (i + lag) % count) for i in range(count)])  5.44 us
    ppermute x4, starting transfers between devices, head_scatter(): lax.ppermute(value, 'head', [(i, i ^ bits) for i in range(count)])  4.52 us
    pallas_call x1, Pallas kernels, local(): pl.pallas_call(scales_kernel, out_shape=(shape((tokens, width), bf16), sh...  3.35 us
  transfers between devices with their start and end apart: 9, of which 2 were waited for; matrix products, arithmetic and copies ran while one was open for 0% of the time, Pallas kernels for 50%

profile of v3, /device:TPU:0, one launch (start us, length us, event | category | flops | bytes accessed | tf_op | source)
XLA Modules:
  0.0 82.9 jit_solution(16277441244103751962)
XLA Ops:
  0.6 0.0 copy-start.3
  0.6 0.0 copy-start.1
  0.7 0.8 shard_map.95
  1.4 0.0 copy-start.2
  1.4 5.0 %collective-permute-start = (bf16[16,1280]{1,0:T(8,128)(2,1)S(1)}, bf16[16,1280]{1,0:T(8,128)(2,1)S(1)}, u32[]{:S(2)}, u32[]{:S(2)}) collective-permute-start(bf16[16,1280]{1,0:T(8,128)(2,1)S(1)} %shard_map.95), channel_id=1, source_target_pairs={{0,8},{8,16},{16,24},{1,9},{9,17},{17,25},{2,10},{10,18},{18,26},{... | collective-permute-start | bytes 122888 | tf_op jit(solution)/shard_map/ppermute | solution.py:548
  6.4 0.0 copy-done.3
  6.4 0.0 copy-done.1
  6.4 3.3 %shard_map.94 = (bf16[1024,256]{1,0:T(8,128)(2,1)S(1)}, f32[32,1024]{1,0:T(8,128)S(1)}, f32[8,1024]{1,0:T(8,128)S(1)}) custom-call(s32[4]{0:T(128)S(1)} %copy-done.1, s32[1]{0:T(128)} %bitcast.start_ref, f32[16,1024]{1,0:T(8,128)S(1)} %copy-done.3), custom_call_target="tpu_custom_call" | custom-call | flops 1048576000 | bytes 16777216 | tf_op jit(solution)/shard_map/pallas_call | solution.py:647
  9.8 0.0 copy-start
  9.8 0.0 collective-permute-done.halo_ref
  9.8 0.0 copy-done.2
  9.8 6.6 %shard_map.96 = (bf16[1024,256]{1,0:T(8,128)(2,1)S(1)}, bf16[1024,256]{1,0:T(8,128)(2,1)S(1)}, f32[1024,256]{1,0:T(8,128)S(1)}, bf16[1024,1024]{1,0:T(8,128)(2,1...) custom-call(s32[4]{0:T(128)S(1)} %copy-done.1, ...), custom_call_target="tpu_custom_call" | custom-call | flops 1048576000 | bytes 16777216 | tf_op jit(solution)/shard_map/pallas_call | solution.py:660
  16.4 0.0 copy-done
  16.4 9.6 %shard_map.97 = (f32[1024,1024]{1,0:T(8,128)S(1)}, bf16[1024,1024]{1,0:T(8,128)(2,1)S(1)}, bf16[1024,1024]{1,0:T(8,128)(2,1)S(1)}, bf16[1024,1024]{1,0:T(8,128)(...) custom-call(s32[4]{0:T(128)S(1)} %copy-done.1, ...), custom_call_target="tpu_custom_call" | custom-call | flops 1048576000 | bytes 16777216 | tf_op jit(solution)/shard_map/pallas_call | solution.py:675
  26.0 1.5 %collective-permute-start.1 = (f32[1032,128]{1,0:T(8,128)S(1)}, f32[1032,128]{1,0:T(8,128)S(1)}, u32[]{:S(2)}, u32[]{:S(2)}) collective-permute-start(f32[1032,128]{1,0:T(8,128)S(1)} %get-tuple-element.55), channel_id=1, source_target_pairs={{0,8},{8,16},{16,24},{24,0},{1,9},{9,17},{17,25},{25,1},{2,10},{10... | collective-permute-start | bytes 1585160 | tf_op jit(solution)/shard_map/ppermute | solution.py:694
  27.6 1.1 %collective-permute-start.2 = (f32[1032,128]{1,0:T(8,128)S(1)}, f32[1032,128]{1,0:T(8,128)S(1)}, u32[]{:S(2)}, u32[]{:S(2)}) collective-permute-start(f32[1032,128]{1,0:T(8,128)S(1)} %get-tuple-element.56), channel_id=1, source_target_pairs={{0,16},{8,24},{16,0},{24,8},{1,17},{9,25},{17,1},{25,9},{2,18},{10... | collective-permute-start | bytes 1585160 | tf_op jit(solution)/shard_map/ppermute | solution.py:694
  28.6 2.8 %collective-permute-start.3 = (f32[1032,128]{1,0:T(8,128)S(1)}, f32[1032,128]{1,0:T(8,128)S(1)}, u32[]{:S(2)}, u32[]{:S(2)}) collective-permute-start(f32[1032,128]{1,0:T(8,128)S(1)} %get-tuple-element.57), channel_id=1, source_target_pairs={{0,24},{8,0},{16,8},{24,16},{1,25},{9,1},{17,9},{25,17},{2,26},{10... | collective-permute-start | bytes 1585160 | tf_op jit(solution)/shard_map/ppermute | solution.py:694
  31.5 23.7 %shard_map.98 = (f32[1024,1024]{1,0:T(8,128)S(1)}, f32[1024,256]{1,0:T(8,128)S(1)}, f32[1024,128]{1,0:T(8,128)S(1)}) custom-call(s32[4]{0:T(128)S(1)} %copy-done.1, s32[1]{0:T(128)} %bitcast.start_ref, f32[32,1024]{1,0:T(8,128)S(1)} %get-tuple-element.47.kappa_ref, bf16[1024,1024]{1,0:T(8,128)(2,1)S(1)} %get-tuple-element.48.fx_h.bx_h, ...), custom_call_target="tpu_custom_call" | custom-call | flops 8388608000 | bytes 16777216 | tf_op jit(solution)/shard_map/pallas_call | solution.py:704
  55.2 0.0 collective-permute-done.1.refs_0_
  55.2 0.0 collective-permute-done.2.refs_1_
  55.2 0.0 collective-permute-done.3.refs_2_
  55.2 0.9 %shard_map.99 = (bf16[256,1024]{1,0:T(8,128)(2,1)S(1)}, bf16[256,1024]{1,0:T(8,128)(2,1)S(1)}, f32[8,1024]{1,0:T(8,128)S(1)}, f32[8,1280]{1,0:T(8,128)S(1)}) custom-call(s32[1]{0:T(128)} %bitcast.start_ref, f32[1032,128]{1,0:T(8,128)S(1)} %collective-permute-done.1.refs_0_, f32[1032,128]{1,0:T(8,128)S(1)} %collective-permute-done.2.refs_1_, ...), custom_call_target="tpu_custom_call" | custom-call | flops 209715200 | bytes 16777216 | tf_op jit(solution)/shard_map/pallas_call | solution.py:719
  56.1 1.5 %collective-permute-start.4 = (f32[8,1280]{1,0:T(8,128)S(1)}, f32[8,1280]{1,0:T(8,128)S(1)}, u32[]{:S(2)}, u32[]{:S(2)}) collective-permute-start(f32[8,1280]{1,0:T(8,128)S(1)} %get-tuple-element.63), channel_id=1, source_target_pairs={{8,0},{16,8},{24,16},{9,1},{17,9},{25,17},{10,2},{18,10},{26,18},{... | collective-permute-start | bytes 122888 | tf_op jit(solution)/shard_map/ppermute | solution.py:548
  57.6 2.6 %shard_map.101.shared_ref = f32[1024,256]{1,0:T(8,128)S(1)} custom-call(bf16[1024,1024]{1,0:T(8,128)(2,1)S(1)} %get-tuple-element.40.refs_4_.gh_ref, bf16[1024,1024]{1,0:T(8,128)(2,1)S(1)} %get-tuple-element.41.refs_5_.gl_ref, bf16[1024,1024]{1,0:T(8,128)(2,1)S(1)} %get-tuple-element.45.refs_6_.xh_ref, ...), custom_call_target="tpu_custom_call" | custom-call | flops 1572864000 | bytes 16777216 | tf_op jit(solution)/shard_map/pallas_call | solution.py:745
  60.2 1.8 %collective-permute-done.4.tail_ref.halo_ref = f32[8,1280]{1,0:T(8,128)S(1)} collective-permute-done((f32[8,1280]{1,0:T(8,128)S(1)}, f32[8,1280]{1,0:T(8,128)S(1)}, u32[]{:S(2)}, u32[]{:S(2)}) %collective-permute-start.4) | collective-permute-done | bytes 40992 | tf_op jit(solution)/shard_map/ppermute | solution.py:548
  62.0 1.5 %shard_map.102 = (f32[512,256]{1,0:T(8,128)S(1)}, f32[512,256]{1,0:T(8,128)S(1)}) custom-call(s32[4]{0:T(128)S(1)} %copy-done.1, s32[1]{0:T(128)} %bitcast.start_ref, s32[1]{0:T(128)} %bitcast.1.side_ref, f32[1024,256]{1,0:T(8,128)S(1)} %shard_map.101.shared_ref, f32[8,1280]{1,0:T(8,128)S(1)} %collective-permute-done.4.tail_ref.halo_ref, f32[4,256]{1,0:T(4,128)S(1)} %copy-done.2), custom_call_target="tpu_custom_call" | custom-call | tf_op jit(solution)/shard_map/pallas_call | solution.py:758
  63.5 0.1 collective-permute-start.5
  63.6 1.9 %collective-permute-done.5.came_ref = f32[4,128,256]{2,1,0:T(8,128)S(1)} collective-permute-done((f32[4,128,256]{2,1,0:T(8,128)S(1)}, f32[4,128,256]{2,1,0:T(8,128)S(1)}, u32[]{:S(2)}, u32[]{:S(2)}) %collective-permute-start.5) | collective-permute-done | bytes 524320 | tf_op jit(solution)/shard_map/ppermute | solution.py:574
  65.5 0.1 shard_map.103
  65.6 1.6 %collective-permute-start.6 = (f32[128,256]{1,0:T(8,128)S(1)}, f32[128,256]{1,0:T(8,128)S(1)}, u32[]{:S(2)}, u32[]{:S(2)}) collective-permute-start(f32[128,256]{1,0:T(8,128)S(1)} %get-tuple-element.69), channel_id=1, source_target_pairs={{0,2},{1,3},{2,0},{3,1},{4,6},{5,7},{6,4},{7,5},{8,10},{9,11},{10,... | collective-permute-start | bytes 393224 | tf_op jit(solution)/shard_map/ppermute | solution.py:574
  67.2 2.6 %collective-permute-start.7 = (f32[128,256]{1,0:T(8,128)S(1)}, f32[128,256]{1,0:T(8,128)S(1)}, u32[]{:S(2)}, u32[]{:S(2)}) collective-permute-start(f32[128,256]{1,0:T(8,128)S(1)} %get-tuple-element.70), channel_id=1, source_target_pairs={{0,4},{1,5},{2,6},{3,7},{4,0},{5,1},{6,2},{7,3},{8,12},{9,13},{10,... | collective-permute-start | bytes 393224 | tf_op jit(solution)/shard_map/ppermute | solution.py:574
  69.8 0.2 collective-permute-start.8
  70.0 12.1 %shard_map.100 = (f32[1024,1024]{1,0:T(8,128)}, f32[16,1024]{1,0:T(8,128)}) custom-call(s32[4]{0:T(128)S(1)} %copy-done.1, s32[1]{0:T(128)} %bitcast.start_ref, bf16[1024,1024]{1,0:T(8,128)(2,1)S(1)} %get-tuple-element.40.refs_4_.gh_ref, bf16[1024,1024]{1,0:T(8,128)(2,1)S(1)} %get-tuple-element.41.refs_5_.gl_ref, ...), custom_call_target="tpu_custom_call" | custom-call | flops 3145728000 | bytes 16777216 | tf_op jit(solution)/shard_map/pallas_call | solution.py:769
  82.2 0.0 collective-permute-done.6.refs_1_
  82.2 0.0 collective-permute-done.7.refs_2_
  82.2 0.0 collective-permute-done.8.refs_3_
  82.2 0.7 shard_map.104
Async XLA Ops:
  0.6 5.8 %copy-start.3 = (f32[16,1024]{1,0:T(8,128)S(1)}, f32[16,1024]{1,0:T(8,128)}, u32[]{:S(2)}) copy-start(f32[16,1024]{1,0:T(8,128)} %log_ref.1) | copy-start | bytes 196612
  0.6 5.8 %copy-start.1 = (s32[4]{0:T(128)S(1)}, s32[4]{0:T(128)}, u32[]{:S(2)}) copy-start(s32[4]{0:T(128)} %lens_ref.11) | copy-start | bytes 52
  1.4 8.4 %copy-start.2 = (f32[4,256]{1,0:T(4,128)S(1)}, f32[4,256]{1,0:T(4,128)}, u32[]{:S(2)}) copy-start(f32[4,256]{1,0:T(4,128)} %taps_ref.7) | copy-start | bytes 12292
  1.4 8.4 %collective-permute-start = (bf16[16,1280]{1,0:T(8,128)(2,1)S(1)}, bf16[16,1280]{1,0:T(8,128)(2,1)S(1)}, u32[]{:S(2)}, u32[]{:S(2)}) collective-permute-start(bf16[16,1280]{1,0:T(8,128)(2,1)S(1)} %shard_map.95), channel_id=1, source_target_pairs={{0,8},{8,16},{16,24},{1,9},{9,17},{17,25},{2,10},{10,18},{18,26},{... | collective-permute-start | bytes 122888 | tf_op jit(solution)/shard_map/ppermute | solution.py:548
  9.8 6.6 %copy-start = (f32[4,1024]{1,0:T(4,128)S(1)}, f32[4,1024]{1,0:T(4,128)}, u32[]{:S(2)}) copy-start(f32[4,1024]{1,0:T(4,128)} %taps_ref.6) | copy-start | bytes 49156
  26.0 29.2 %collective-permute-start.1 = (f32[1032,128]{1,0:T(8,128)S(1)}, f32[1032,128]{1,0:T(8,128)S(1)}, u32[]{:S(2)}, u32[]{:S(2)}) collective-permute-start(f32[1032,128]{1,0:T(8,128)S(1)} %get-tuple-element.55), channel_id=1, source_target_pairs={{0,8},{8,16},{16,24},{24,0},{1,9},{9,17},{17,25},{25,1},{2,10},{10... | collective-permute-start | bytes 1585160 | tf_op jit(solution)/shard_map/ppermute | solution.py:694
  27.6 27.6 %collective-permute-start.2 = (f32[1032,128]{1,0:T(8,128)S(1)}, f32[1032,128]{1,0:T(8,128)S(1)}, u32[]{:S(2)}, u32[]{:S(2)}) collective-permute-start(f32[1032,128]{1,0:T(8,128)S(1)} %get-tuple-element.56), channel_id=1, source_target_pairs={{0,16},{8,24},{16,0},{24,8},{1,17},{9,25},{17,1},{25,9},{2,18},{10... | collective-permute-start | bytes 1585160 | tf_op jit(solution)/shard_map/ppermute | solution.py:694
  28.6 26.6 %collective-permute-start.3 = (f32[1032,128]{1,0:T(8,128)S(1)}, f32[1032,128]{1,0:T(8,128)S(1)}, u32[]{:S(2)}, u32[]{:S(2)}) collective-permute-start(f32[1032,128]{1,0:T(8,128)S(1)} %get-tuple-element.57), channel_id=1, source_target_pairs={{0,24},{8,0},{16,8},{24,16},{1,25},{9,1},{17,9},{25,17},{2,26},{10... | collective-permute-start | bytes 1585160 | tf_op jit(solution)/shard_map/ppermute | solution.py:694
  56.1 5.9 %collective-permute-start.4 = (f32[8,1280]{1,0:T(8,128)S(1)}, f32[8,1280]{1,0:T(8,128)S(1)}, u32[]{:S(2)}, u32[]{:S(2)}) collective-permute-start(f32[8,1280]{1,0:T(8,128)S(1)} %get-tuple-element.63), channel_id=1, source_target_pairs={{8,0},{16,8},{24,16},{9,1},{17,9},{25,17},{10,2},{18,10},{26,18},{... | collective-permute-start | bytes 122888 | tf_op jit(solution)/shard_map/ppermute | solution.py:548
  63.5 2.0 %collective-permute-start.5 = (f32[4,128,256]{2,1,0:T(8,128)S(1)}, f32[4,128,256]{2,1,0:T(8,128)S(1)}, u32[]{:S(2)}, u32[]{:S(2)}) collective-permute-start(f32[4,128,256]{2,1,0:T(8,128)S(1)} %bitcast.5), channel_id=1, source_target_pairs={{0,1},{1,0},{2,3},{3,2},{4,5},{5,4},{6,7},{7,6},{8,9},{9,8},{10,11... | collective-permute-start | bytes 1572872 | tf_op jit(solution)/shard_map/ppermute | solution.py:574
  65.6 16.6 %collective-permute-start.6 = (f32[128,256]{1,0:T(8,128)S(1)}, f32[128,256]{1,0:T(8,128)S(1)}, u32[]{:S(2)}, u32[]{:S(2)}) collective-permute-start(f32[128,256]{1,0:T(8,128)S(1)} %get-tuple-element.69), channel_id=1, source_target_pairs={{0,2},{1,3},{2,0},{3,1},{4,6},{5,7},{6,4},{7,5},{8,10},{9,11},{10,... | collective-permute-start | bytes 393224 | tf_op jit(solution)/shard_map/ppermute | solution.py:574
  67.2 15.0 %collective-permute-start.7 = (f32[128,256]{1,0:T(8,128)S(1)}, f32[128,256]{1,0:T(8,128)S(1)}, u32[]{:S(2)}, u32[]{:S(2)}) collective-permute-start(f32[128,256]{1,0:T(8,128)S(1)} %get-tuple-element.70), channel_id=1, source_target_pairs={{0,4},{1,5},{2,6},{3,7},{4,0},{5,1},{6,2},{7,3},{8,12},{9,13},{10,... | collective-permute-start | bytes 393224 | tf_op jit(solution)/shard_map/ppermute | solution.py:574
  69.8 12.4 %collective-permute-start.8 = (f32[128,256]{1,0:T(8,128)S(1)}, f32[128,256]{1,0:T(8,128)S(1)}, u32[]{:S(2)}, u32[]{:S(2)}) collective-permute-start(f32[128,256]{1,0:T(8,128)S(1)} %get-tuple-element.71), channel_id=1, source_target_pairs={{0,6},{1,7},{2,4},{3,5},{4,2},{5,3},{6,0},{7,1},{8,14},{9,15},{10,... | collective-permute-start | bytes 393224 | tf_op jit(solution)/shard_map/ppermute | solution.py:574

commit v4 on v3

--- a/solution.py
+++ b/solution.py
@@ -531,15 +531,15 @@
     log_ref[...] = log[0:heads, :]
     carry[...] += sums[:, rows:]
     first = start_ref[0] + (pl.num_programs(0) - 1 - step) * rows
-
-    def body(link):
-        for r in range(0, rows, 64):
-            at, linked = slice(r, r + 64), link(r, 64)
+    for r in range(0, rows, 64):
+
+        def body(link, at=slice(r, r + 64)):
+            linked = link(0, 64)
             for c in range(0, channels, LANES):
                 over = slice(c, c + LANES)
-                out_ref[at, over] = conv_tile(ext, taps_ref, r, 64, over, linked, 1)
-
-    two_ways(first, rows, 1, lens_ref, body)
+                out_ref[at, over] = conv_tile(ext, taps_ref, at.start, 64, over, linked, 1)
+
+        two_ways(first + r, 64, 1, lens_ref, body)
 
 
 def shifted(value, axis, steps):
@@ -741,7 +741,7 @@
     )
     after = shifted(head, "seq", -1)
 
-    high = 512
+    high = tokens
     shared = pl.pallas_call(
         shared_kernel,
         grid=(tokens // high,),

time: 83 us -> 81.3 us (0.980)
  starting transfers between devices: 16.4 us -> 14.5 us
    ppermute x3, starting transfers between devices: 5.44 us -> 3.56 us  [local(): lax.ppermute(message, 'seq', [(i, (i + lag) % count) for i in range(count)])]
  transfers between devices with their start and end apart: 9 -> 9, of which waited for: 2 -> 2; matrix products, arithmetic and copies ran while one was open for 0% -> 0% of each run, Pallas kernels for 50% -> 51%
where the time goes in v4:
time: 81.3 us; the launch traced here: 80.8 us
  Pallas kernels  61.5 us (76%)
  starting transfers between devices  14.5 us (18%)
  waiting for transfers between devices  3.9 us (5%)
  between operations  0.82 us (1%)
    pallas_call x1, Pallas kernels, local(): pl.pallas_call(functools.partial(local_kernel, heads=heads), grid=(chunks...  23.7 us
    pallas_call x1, Pallas kernels, local(): pl.pallas_call(functools.partial(final_kernel, heads=heads), grid=(steps,...  11.9 us
    pallas_call x1, Pallas kernels, local(): pl.pallas_call(functools.partial(state_kernel, heads=heads, count=count),...  9.61 us
    pallas_call x1, Pallas kernels, local(): pl.pallas_call(functools.partial(adjoint_kernel, heads=heads), grid=(step...  6.57 us
    ppermute x2, starting transfers between devices, shifted(): lax.ppermute(value, axis, [(source, source + steps) for source in range(i...  6.44 us
    ppermute x4, starting transfers between devices, head_scatter(): lax.ppermute(value, 'head', [(i, i ^ bits) for i in range(count)])  4.52 us
    ppermute x3, starting transfers between devices, local(): lax.ppermute(message, 'seq', [(i, (i + lag) % count) for i in range(count)])  3.56 us
    pallas_call x1, Pallas kernels, local(): pl.pallas_call(scales_kernel, out_shape=(shape((tokens, width), bf16), sh...  3.35 us
  transfers between devices with their start and end apart: 9, of which 2 were waited for; matrix products, arithmetic and copies ran while one was open for 0% of the time, Pallas kernels for 51%

profile of v4, /device:TPU:0, one launch (start us, length us, event | category | flops | bytes accessed | tf_op | source)
XLA Modules:
  0.0 80.8 jit_solution(7750444023232124699)
XLA Ops:
  0.6 0.0 copy-start.3
  0.6 0.0 copy-start.1
  0.7 0.8 shard_map.95
  1.4 0.0 copy-start.2
  1.4 5.0 %collective-permute-start = (bf16[16,1280]{1,0:T(8,128)(2,1)S(1)}, bf16[16,1280]{1,0:T(8,128)(2,1)S(1)}, u32[]{:S(2)}, u32[]{:S(2)}) collective-permute-start(bf16[16,1280]{1,0:T(8,128)(2,1)S(1)} %shard_map.95), channel_id=1, source_target_pairs={{0,8},{8,16},{16,24},{1,9},{9,17},{17,25},{2,10},{10,18},{18,26},{... | collective-permute-start | bytes 122888 | tf_op jit(solution)/shard_map/ppermute | solution.py:548
  6.4 0.0 copy-done.3
  6.4 0.0 copy-done.1
  6.4 3.3 %shard_map.94 = (bf16[1024,256]{1,0:T(8,128)(2,1)S(1)}, f32[32,1024]{1,0:T(8,128)S(1)}, f32[8,1024]{1,0:T(8,128)S(1)}) custom-call(s32[4]{0:T(128)S(1)} %copy-done.1, s32[1]{0:T(128)} %bitcast.start_ref, f32[16,1024]{1,0:T(8,128)S(1)} %copy-done.3), custom_call_target="tpu_custom_call" | custom-call | flops 1048576000 | bytes 16777216 | tf_op jit(solution)/shard_map/pallas_call | solution.py:647
  9.8 0.0 copy-start
  9.8 0.0 collective-permute-done.halo_ref
  9.8 0.0 copy-done.2
  9.8 6.6 %shard_map.96 = (bf16[1024,256]{1,0:T(8,128)(2,1)S(1)}, bf16[1024,256]{1,0:T(8,128)(2,1)S(1)}, f32[1024,256]{1,0:T(8,128)S(1)}, bf16[1024,1024]{1,0:T(8,128)(2,1...) custom-call(s32[4]{0:T(128)S(1)} %copy-done.1, ...), custom_call_target="tpu_custom_call" | custom-call | flops 1048576000 | bytes 16777216 | tf_op jit(solution)/shard_map/pallas_call | solution.py:660
  16.4 0.0 copy-done
  16.4 9.6 %shard_map.97 = (f32[1024,1024]{1,0:T(8,128)S(1)}, bf16[1024,1024]{1,0:T(8,128)(2,1)S(1)}, bf16[1024,1024]{1,0:T(8,128)(2,1)S(1)}, bf16[1024,1024]{1,0:T(8,128)(...) custom-call(s32[4]{0:T(128)S(1)} %copy-done.1, ...), custom_call_target="tpu_custom_call" | custom-call | flops 1048576000 | bytes 16777216 | tf_op jit(solution)/shard_map/pallas_call | solution.py:675
  26.0 1.5 %collective-permute-start.1 = (f32[1032,128]{1,0:T(8,128)S(1)}, f32[1032,128]{1,0:T(8,128)S(1)}, u32[]{:S(2)}, u32[]{:S(2)}) collective-permute-start(f32[1032,128]{1,0:T(8,128)S(1)} %get-tuple-element.55), channel_id=1, source_target_pairs={{0,8},{8,16},{16,24},{24,0},{1,9},{9,17},{17,25},{25,1},{2,10},{10... | collective-permute-start | bytes 1585160 | tf_op jit(solution)/shard_map/ppermute | solution.py:694
  27.6 0.6 collective-permute-start.2
  28.2 1.4 %collective-permute-start.3 = (f32[1032,128]{1,0:T(8,128)S(1)}, f32[1032,128]{1,0:T(8,128)S(1)}, u32[]{:S(2)}, u32[]{:S(2)}) collective-permute-start(f32[1032,128]{1,0:T(8,128)S(1)} %get-tuple-element.57), channel_id=1, source_target_pairs={{0,24},{8,0},{16,8},{24,16},{1,25},{9,1},{17,9},{25,17},{2,26},{10... | collective-permute-start | bytes 1585160 | tf_op jit(solution)/shard_map/ppermute | solution.py:694
  29.6 23.7 %shard_map.98 = (f32[1024,1024]{1,0:T(8,128)S(1)}, f32[1024,256]{1,0:T(8,128)S(1)}, f32[1024,128]{1,0:T(8,128)S(1)}) custom-call(s32[4]{0:T(128)S(1)} %copy-done.1, s32[1]{0:T(128)} %bitcast.start_ref, f32[32,1024]{1,0:T(8,128)S(1)} %get-tuple-element.47.kappa_ref, bf16[1024,1024]{1,0:T(8,128)(2,1)S(1)} %get-tuple-element.48.fx_h.bx_h, ...), custom_call_target="tpu_custom_call" | custom-call | flops 8388608000 | bytes 16777216 | tf_op jit(solution)/shard_map/pallas_call | solution.py:704
  53.3 0.0 collective-permute-done.1.refs_0_
  53.3 0.0 collective-permute-done.2.refs_1_
  53.3 0.0 collective-permute-done.3.refs_2_
  53.3 0.9 %shard_map.99 = (bf16[256,1024]{1,0:T(8,128)(2,1)S(1)}, bf16[256,1024]{1,0:T(8,128)(2,1)S(1)}, f32[8,1024]{1,0:T(8,128)S(1)}, f32[8,1280]{1,0:T(8,128)S(1)}) custom-call(s32[1]{0:T(128)} %bitcast.start_ref, f32[1032,128]{1,0:T(8,128)S(1)} %collective-permute-done.1.refs_0_, f32[1032,128]{1,0:T(8,128)S(1)} %collective-permute-done.2.refs_1_, ...), custom_call_target="tpu_custom_call" | custom-call | flops 209715200 | bytes 16777216 | tf_op jit(solution)/shard_map/pallas_call | solution.py:719
  54.2 1.5 %collective-permute-start.4 = (f32[8,1280]{1,0:T(8,128)S(1)}, f32[8,1280]{1,0:T(8,128)S(1)}, u32[]{:S(2)}, u32[]{:S(2)}) collective-permute-start(f32[8,1280]{1,0:T(8,128)S(1)} %get-tuple-element.63), channel_id=1, source_target_pairs={{8,0},{16,8},{24,16},{9,1},{17,9},{25,17},{10,2},{18,10},{26,18},{... | collective-permute-start | bytes 122888 | tf_op jit(solution)/shard_map/ppermute | solution.py:548
  55.7 2.4 %shard_map.101.shared_ref = f32[1024,256]{1,0:T(8,128)S(1)} custom-call(bf16[1024,1024]{1,0:T(8,128)(2,1)S(1)} %get-tuple-element.40.refs_4_.gh_ref, bf16[1024,1024]{1,0:T(8,128)(2,1)S(1)} %get-tuple-element.41.refs_5_.gl_ref, bf16[1024,1024]{1,0:T(8,128)(2,1)S(1)} %get-tuple-element.45.refs_6_.xh_ref, ...), custom_call_target="tpu_custom_call" | custom-call | flops 1572864000 | bytes 16777216 | tf_op jit(solution)/shard_map/pallas_call | solution.py:745
  58.2 2.0 %collective-permute-done.4.tail_ref.halo_ref = f32[8,1280]{1,0:T(8,128)S(1)} collective-permute-done((f32[8,1280]{1,0:T(8,128)S(1)}, f32[8,1280]{1,0:T(8,128)S(1)}, u32[]{:S(2)}, u32[]{:S(2)}) %collective-permute-start.4) | collective-permute-done | bytes 40992 | tf_op jit(solution)/shard_map/ppermute | solution.py:548
  60.1 1.5 %shard_map.102 = (f32[512,256]{1,0:T(8,128)S(1)}, f32[512,256]{1,0:T(8,128)S(1)}) custom-call(s32[4]{0:T(128)S(1)} %copy-done.1, s32[1]{0:T(128)} %bitcast.start_ref, s32[1]{0:T(128)} %bitcast.1.side_ref, f32[1024,256]{1,0:T(8,128)S(1)} %shard_map.101.shared_ref, f32[8,1280]{1,0:T(8,128)S(1)} %collective-permute-done.4.tail_ref.halo_ref, f32[4,256]{1,0:T(4,128)S(1)} %copy-done.2), custom_call_target="tpu_custom_call" | custom-call | tf_op jit(solution)/shard_map/pallas_call | solution.py:758
  61.6 0.1 collective-permute-start.5
  61.7 1.9 %collective-permute-done.5.came_ref = f32[4,128,256]{2,1,0:T(8,128)S(1)} collective-permute-done((f32[4,128,256]{2,1,0:T(8,128)S(1)}, f32[4,128,256]{2,1,0:T(8,128)S(1)}, u32[]{:S(2)}, u32[]{:S(2)}) %collective-permute-start.5) | collective-permute-done | bytes 524320 | tf_op jit(solution)/shard_map/ppermute | solution.py:574
  63.6 0.1 shard_map.103
  63.7 1.6 %collective-permute-start.6 = (f32[128,256]{1,0:T(8,128)S(1)}, f32[128,256]{1,0:T(8,128)S(1)}, u32[]{:S(2)}, u32[]{:S(2)}) collective-permute-start(f32[128,256]{1,0:T(8,128)S(1)} %get-tuple-element.69), channel_id=1, source_target_pairs={{0,2},{1,3},{2,0},{3,1},{4,6},{5,7},{6,4},{7,5},{8,10},{9,11},{10,... | collective-permute-start | bytes 393224 | tf_op jit(solution)/shard_map/ppermute | solution.py:574
  65.3 2.6 %collective-permute-start.7 = (f32[128,256]{1,0:T(8,128)S(1)}, f32[128,256]{1,0:T(8,128)S(1)}, u32[]{:S(2)}, u32[]{:S(2)}) collective-permute-start(f32[128,256]{1,0:T(8,128)S(1)} %get-tuple-element.70), channel_id=1, source_target_pairs={{0,4},{1,5},{2,6},{3,7},{4,0},{5,1},{6,2},{7,3},{8,12},{9,13},{10,... | collective-permute-start | bytes 393224 | tf_op jit(solution)/shard_map/ppermute | solution.py:574
  67.9 0.2 collective-permute-start.8
  68.1 11.9 %shard_map.100 = (f32[1024,1024]{1,0:T(8,128)}, f32[16,1024]{1,0:T(8,128)}) custom-call(s32[4]{0:T(128)S(1)} %copy-done.1, s32[1]{0:T(128)} %bitcast.start_ref, bf16[1024,1024]{1,0:T(8,128)(2,1)S(1)} %get-tuple-element.40.refs_4_.gh_ref, bf16[1024,1024]{1,0:T(8,128)(2,1)S(1)} %get-tuple-element.41.refs_5_.gl_ref, ...), custom_call_target="tpu_custom_call" | custom-call | flops 3145728000 | bytes 16777216 | tf_op jit(solution)/shard_map/pallas_call | solution.py:769
  80.1 0.0 collective-permute-done.6.refs_1_
  80.1 0.0 collective-permute-done.7.refs_2_
  80.1 0.0 collective-permute-done.8.refs_3_
  80.1 0.7 shard_map.104
Async XLA Ops:
  0.6 5.8 %copy-start.3 = (f32[16,1024]{1,0:T(8,128)S(1)}, f32[16,1024]{1,0:T(8,128)}, u32[]{:S(2)}) copy-start(f32[16,1024]{1,0:T(8,128)} %log_ref.1) | copy-start | bytes 196612
  0.6 5.8 %copy-start.1 = (s32[4]{0:T(128)S(1)}, s32[4]{0:T(128)}, u32[]{:S(2)}) copy-start(s32[4]{0:T(128)} %lens_ref.11) | copy-start | bytes 52
  1.4 8.4 %copy-start.2 = (f32[4,256]{1,0:T(4,128)S(1)}, f32[4,256]{1,0:T(4,128)}, u32[]{:S(2)}) copy-start(f32[4,256]{1,0:T(4,128)} %taps_ref.7) | copy-start | bytes 12292
  1.4 8.4 %collective-permute-start = (bf16[16,1280]{1,0:T(8,128)(2,1)S(1)}, bf16[16,1280]{1,0:T(8,128)(2,1)S(1)}, u32[]{:S(2)}, u32[]{:S(2)}) collective-permute-start(bf16[16,1280]{1,0:T(8,128)(2,1)S(1)} %shard_map.95), channel_id=1, source_target_pairs={{0,8},{8,16},{16,24},{1,9},{9,17},{17,25},{2,10},{10,18},{18,26},{... | collective-permute-start | bytes 122888 | tf_op jit(solution)/shard_map/ppermute | solution.py:548
  9.8 6.6 %copy-start = (f32[4,1024]{1,0:T(4,128)S(1)}, f32[4,1024]{1,0:T(4,128)}, u32[]{:S(2)}) copy-start(f32[4,1024]{1,0:T(4,128)} %taps_ref.6) | copy-start | bytes 49156
  26.0 27.3 %collective-permute-start.1 = (f32[1032,128]{1,0:T(8,128)S(1)}, f32[1032,128]{1,0:T(8,128)S(1)}, u32[]{:S(2)}, u32[]{:S(2)}) collective-permute-start(f32[1032,128]{1,0:T(8,128)S(1)} %get-tuple-element.55), channel_id=1, source_target_pairs={{0,8},{8,16},{16,24},{24,0},{1,9},{9,17},{17,25},{25,1},{2,10},{10... | collective-permute-start | bytes 1585160 | tf_op jit(solution)/shard_map/ppermute | solution.py:694
  27.6 25.7 %collective-permute-start.2 = (f32[1032,128]{1,0:T(8,128)S(1)}, f32[1032,128]{1,0:T(8,128)S(1)}, u32[]{:S(2)}, u32[]{:S(2)}) collective-permute-start(f32[1032,128]{1,0:T(8,128)S(1)} %get-tuple-element.56), channel_id=1, source_target_pairs={{0,16},{8,24},{16,0},{24,8},{1,17},{9,25},{17,1},{25,9},{2,18},{10... | collective-permute-start | bytes 1585160 | tf_op jit(solution)/shard_map/ppermute | solution.py:694
  28.2 25.2 %collective-permute-start.3 = (f32[1032,128]{1,0:T(8,128)S(1)}, f32[1032,128]{1,0:T(8,128)S(1)}, u32[]{:S(2)}, u32[]{:S(2)}) collective-permute-start(f32[1032,128]{1,0:T(8,128)S(1)} %get-tuple-element.57), channel_id=1, source_target_pairs={{0,24},{8,0},{16,8},{24,16},{1,25},{9,1},{17,9},{25,17},{2,26},{10... | collective-permute-start | bytes 1585160 | tf_op jit(solution)/shard_map/ppermute | solution.py:694
  54.2 5.9 %collective-permute-start.4 = (f32[8,1280]{1,0:T(8,128)S(1)}, f32[8,1280]{1,0:T(8,128)S(1)}, u32[]{:S(2)}, u32[]{:S(2)}) collective-permute-start(f32[8,1280]{1,0:T(8,128)S(1)} %get-tuple-element.63), channel_id=1, source_target_pairs={{8,0},{16,8},{24,16},{9,1},{17,9},{25,17},{10,2},{18,10},{26,18},{... | collective-permute-start | bytes 122888 | tf_op jit(solution)/shard_map/ppermute | solution.py:548
  61.6 2.0 %collective-permute-start.5 = (f32[4,128,256]{2,1,0:T(8,128)S(1)}, f32[4,128,256]{2,1,0:T(8,128)S(1)}, u32[]{:S(2)}, u32[]{:S(2)}) collective-permute-start(f32[4,128,256]{2,1,0:T(8,128)S(1)} %bitcast.5), channel_id=1, source_target_pairs={{0,1},{1,0},{2,3},{3,2},{4,5},{5,4},{6,7},{7,6},{8,9},{9,8},{10,11... | collective-permute-start | bytes 1572872 | tf_op jit(solution)/shard_map/ppermute | solution.py:574
  63.7 16.4 %collective-permute-start.6 = (f32[128,256]{1,0:T(8,128)S(1)}, f32[128,256]{1,0:T(8,128)S(1)}, u32[]{:S(2)}, u32[]{:S(2)}) collective-permute-start(f32[128,256]{1,0:T(8,128)S(1)} %get-tuple-element.69), channel_id=1, source_target_pairs={{0,2},{1,3},{2,0},{3,1},{4,6},{5,7},{6,4},{7,5},{8,10},{9,11},{10,... | collective-permute-start | bytes 393224 | tf_op jit(solution)/shard_map/ppermute | solution.py:574
  65.3 14.8 %collective-permute-start.7 = (f32[128,256]{1,0:T(8,128)S(1)}, f32[128,256]{1,0:T(8,128)S(1)}, u32[]{:S(2)}, u32[]{:S(2)}) collective-permute-start(f32[128,256]{1,0:T(8,128)S(1)} %get-tuple-element.70), channel_id=1, source_target_pairs={{0,4},{1,5},{2,6},{3,7},{4,0},{5,1},{6,2},{7,3},{8,12},{9,13},{10,... | collective-permute-start | bytes 393224 | tf_op jit(solution)/shard_map/ppermute | solution.py:574
  67.9 12.2 %collective-permute-start.8 = (f32[128,256]{1,0:T(8,128)S(1)}, f32[128,256]{1,0:T(8,128)S(1)}, u32[]{:S(2)}, u32[]{:S(2)}) collective-permute-start(f32[128,256]{1,0:T(8,128)S(1)} %get-tuple-element.71), channel_id=1, source_target_pairs={{0,6},{1,7},{2,4},{3,5},{4,2},{5,3},{6,0},{7,1},{8,14},{9,15},{10,... | collective-permute-start | bytes 393224 | tf_op jit(solution)/shard_map/ppermute | solution.py:574
